TPU v7x, 32 devices: a whole 2x2x4 slice. The times are simulated.
32 devices in a mesh: tm: 8 (over z, x), space: 4 (over y, core).
Axes of the slice: x: 2, y: 2, z: 4, core: 2. Of those that a mesh axis runs over, the one named last changes fastest.
Arguments:
- source: float32 [64, 8, 128, 128], P('tm', 'space'), may hold values from -6 to 6
- thrust_axial: float32 [8, 128, 128], P('space'), may hold values from -6 to 6
- thrust_lateral: float32 [8, 128, 128], P('space'), may hold values from -6 to 6
- yaw_index: int32 [16], P('tm'), may hold values from 0 to 23
- diffusivity: float32 [8, 128, 128], P('space'), may hold values from 0.5 to 1
- cotangent: float32 [64, 8, 128, 128], P('tm', 'space'), may hold values from -6 to 6
Outputs:
- forward_state: float32 [64, 8, 128, 128], P('tm', 'space')
- adjoint_state: float32 [64, 8, 128, 128], P('tm', 'space')
All inputs are finite; a program needn't handle non-finite values.
Results may differ from a plain program's by a relative error of at most 0.00002.
Values sent between devices are 32-bit elements; how exact they have to be, the bound alone decides.
A program may use at most 64 MiB of HBM per device.

v0:
```python
import math

import jax
import jax.numpy as jnp
from jax import lax
from jax.sharding import PartitionSpec as P

YAWS = 24


tau_levels = (0.03, 0.06, 0.08)
drift_x = 0.3
drift_y = 0.2


def extended(shard, sides, width):
    for axis, dim in sides:
        count, length = (lax.axis_size(axis), shard.shape[dim])
        up = [(i, (i + 1) % count) for i in range(count - 1)]
        down = [(j, i) for i, j in up]
        last = lax.slice_in_dim(shard, length - width, length, axis=dim)
        leading = lax.slice_in_dim(shard, 0, width, axis=dim)
        before = lax.ppermute(last, axis, up)
        after = lax.ppermute(leading, axis, down)
        shard = jnp.concatenate([before, shard, after], axis=dim)
    return shard


def shifted(block, axis, distance):
    devices = range(lax.axis_size(axis))
    route = [(i - distance, i) for i in devices if i - distance in devices]
    return lax.ppermute(block, axis, route)


def second_diff(padded):
    centre = padded[:, :, 1:-1]
    neighbours = padded[:, :, 2:] + padded[:, :, :-2]
    neighbours = neighbours + jnp.roll(centre, 1, 3) + jnp.roll(centre, -1, 3)
    neighbours = neighbours + jnp.roll(centre, 1, 4) + jnp.roll(centre, -1, 4)
    return neighbours - 6.0 * centre


def drift(field):
    along_x = jnp.roll(field, -1, 4) - jnp.roll(field, 1, 4)
    along_y = jnp.roll(field, -1, 3) - jnp.roll(field, 1, 3)
    return 0.5 * drift_x * along_x + 0.5 * drift_y * along_y


def propagate(paired, diffusivity, depth_level):
    step_size = tau_levels[depth_level]
    sent = jnp.stack([paired[0], diffusivity * paired[1]])
    padded = extended(sent, (("space", 2),), 1)
    curvature = second_diff(padded)
    slopes = drift(paired)
    forward = paired[0] + step_size * (diffusivity * curvature[0]) - step_size * slopes[0]
    adjoint = paired[1] + step_size * curvature[1] + step_size * slopes[1]
    return jnp.stack([forward, adjoint])


def neighbour_pass(paired, distance):
    later = shifted(paired[0], "tm", distance)
    earlier = shifted(paired[1], "tm", -distance)
    return jnp.stack([later, earlier])


def chain_pass(paired, distance):
    later = shifted(paired[0], "tm", distance)
    earlier = shifted(paired[1], "tm", -distance)
    return jnp.stack([later, earlier])


def on_device(source, thrust_axial, thrust_lateral, yaw_index, diffusivity, cotangent):
    blocks = yaw_index.shape[0]
    grid = source.shape[1:]
    angle = 2.0 * math.pi / YAWS * yaw_index.astype(jnp.float32)
    push = (
        jnp.cos(angle)[:, None, None, None] * thrust_axial
        + jnp.sin(angle)[:, None, None, None] * thrust_lateral
    )
    forward_rhs = source.reshape((blocks, 4) + grid) + push[:, None]
    adjoint_rhs = cotangent[::-1].reshape((blocks, 4) + grid)
    rhs_pair = jnp.stack([forward_rhs, adjoint_rhs])
    device = lax.axis_index("tm")
    members = lax.axis_size("tm")
    position = jnp.stack([device, members - 1 - device])
    odd_mask = (position % 2 == 1).reshape(2, 1, 1, 1, 1)
    marched = rhs_pair[:, :, 0]
    marched = propagate(marched, diffusivity, 0) + rhs_pair[:, :, 1]
    marched = propagate(marched, diffusivity, 0) + rhs_pair[:, :, 2]
    residual = propagate(marched, diffusivity, 0) + rhs_pair[:, :, 3]
    coarse_head = residual[:, 0:1]
    coarse_tail = residual[:, 1:2]
    advanced = propagate(coarse_head, diffusivity, 1) + coarse_tail
    inbound = neighbour_pass(advanced, 1)
    middle = propagate(inbound, diffusivity, 1) + coarse_head
    coarse_rhs = propagate(middle, diffusivity, 1) + coarse_tail
    pulled = jnp.where(odd_mask, 0.0, chain_pass(coarse_rhs, -1))
    chain_value = pulled

    def relay_turn(turn, carried):
        updated = propagate(chain_pass(carried, 2), diffusivity, 2) + pulled
        return jnp.where(odd_mask, 0.0, updated)

    chain_value = lax.fori_loop(0, members // 2 - 1, relay_turn, chain_value)
    previous = chain_pass(chain_value, 2)
    handed = chain_pass(chain_value, 1)
    coarse = jnp.where(odd_mask, handed, previous)
    leading = propagate(coarse, diffusivity, 1) + coarse_head
    second = propagate(leading, diffusivity, 1) + coarse_tail
    inbound_two = neighbour_pass(second, 1)
    trailing = propagate(inbound_two, diffusivity, 1) + coarse_head
    level_head = jnp.where(odd_mask, trailing, leading)
    level_tail = jnp.where(odd_mask, coarse, second)
    before = neighbour_pass(level_tail, 1)
    starts = jnp.concatenate([before, level_head], 1)
    fine_first = propagate(starts, diffusivity, 0) + rhs_pair[:, :, 0]
    fine_second = propagate(fine_first, diffusivity, 0) + rhs_pair[:, :, 1]
    fine_third = propagate(fine_second, diffusivity, 0) + rhs_pair[:, :, 2]
    level_values = jnp.concatenate([level_head, level_tail], 1)
    points = jnp.stack([fine_first, fine_second, fine_third, level_values], 2)
    points = points.reshape((2, blocks * 4) + grid)
    return (points[0], points[1][::-1])


def solution(mesh):
    return jax.shard_map(
        on_device,
        mesh=mesh,
        in_specs=(
            P("tm", "space", None, None),
            P("space", None, None),
            P("space", None, None),
            P("tm"),
            P("space", None, None),
            P("tm", "space", None, None),
        ),
        out_specs=(P("tm", "space", None, None), P("tm", "space", None, None)),
        check_vma=False,
    )
```

profile of v0, /device:TPU:1, one launch (start us, length us, event | category | flops | bytes accessed | tf_op | source)
XLA Modules:
  0.0 234.3 jit_solution(7797295826963992711)
XLA Ops:
  4.1 2.0 collective-permute-start.4
  6.1 4.5 %collective-permute-start.5 = (f32[2,2,1,128,128]{4,3,2,1,0:T(8,128)S(1)}, f32[2,2,1,128,128]{4,3,2,1,0:T(8,128)S(1)}, u32[]{:S(2)}, u32[]{:S(2)}) collective-permute-start(f32[2,2,1,128,128]{4,3,2,1,0:T(8,128)S(1)} %get-tuple-element.214), channel_id=1, source_target_pairs={{0,1},{1,2},{2,3},{4,5},{5,6},{6,7},{8,9},{9,10},{10,11},{12,13},{... | collective-permute-start | bytes 786440 | tf_op jit(solution)/shard_map/ppermute | solution.py:23
  17.5 4.4 %collective-permute-start.7 = (f32[2,2,1,128,128]{4,3,2,1,0:T(8,128)S(1)}, f32[2,2,1,128,128]{4,3,2,1,0:T(8,128)S(1)}, u32[]{:S(2)}, u32[]{:S(2)}) collective-permute-start(f32[2,2,1,128,128]{4,3,2,1,0:T(8,128)S(1)} %get-tuple-element.194), channel_id=1, source_target_pairs={{0,1},{1,2},{2,3},{4,5},{5,6},{6,7},{8,9},{9,10},{10,11},{12,13},{... | collective-permute-start | bytes 786440 | tf_op jit(solution)/shard_map/ppermute | solution.py:23
  28.8 4.4 %collective-permute-start.9 = (f32[2,2,1,128,128]{4,3,2,1,0:T(8,128)S(1)}, f32[2,2,1,128,128]{4,3,2,1,0:T(8,128)S(1)}, u32[]{:S(2)}, u32[]{:S(2)}) collective-permute-start(f32[2,2,1,128,128]{4,3,2,1,0:T(8,128)S(1)} %get-tuple-element.174), channel_id=1, source_target_pairs={{0,1},{1,2},{2,3},{4,5},{5,6},{6,7},{8,9},{9,10},{10,11},{12,13},{... | collective-permute-start | bytes 786440 | tf_op jit(solution)/shard_map/ppermute | solution.py:23
  39.8 4.4 %collective-permute-start.11 = (f32[2,1,1,128,128]{4,3,2,1,0:T(8,128)S(1)}, f32[2,1,1,128,128]{4,3,2,1,0:T(8,128)S(1)}, u32[]{:S(2)}, u32[]{:S(2)}) collective-permute-start(f32[2,1,1,128,128]{4,3,2,1,0:T(8,128)S(1)} %get-tuple-element.326), channel_id=1, source_target_pairs={{0,1},{1,2},{2,3},{4,5},{5,6},{6,7},{8,9},{9,10},{10,11},{12,13},{... | collective-permute-start | bytes 393224 | tf_op jit(solution)/shard_map/ppermute | solution.py:23
  47.8 4.0 %collective-permute-start.12 = (f32[1,2,128,128]{3,2,1,0:T(8,128)S(1)}, f32[1,2,128,128]{3,2,1,0:T(8,128)S(1)}, u32[]{:S(2)}, u32[]{:S(2)}) collective-permute-start(f32[1,2,128,128]{3,2,1,0:T(8,128)S(1)} %get-tuple-element.315), channel_id=1, source_target_pairs={{0,4},{4,8},{8,12},{12,16},{16,20},{20,24},{24,28},{1,5},{5,9},{9,... | collective-permute-start | bytes 393224 | tf_op jit(solution)/shard_map/ppermute | solution.py:32
  52.3 2.1 collective-permute-done.12
  56.7 4.9 %collective-permute-start.15 = (f32[2,1,1,128,128]{4,3,2,1,0:T(8,128)S(1)}, f32[2,1,1,128,128]{4,3,2,1,0:T(8,128)S(1)}, u32[]{:S(2)}, u32[]{:S(2)}) collective-permute-start(f32[2,1,1,128,128]{4,3,2,1,0:T(8,128)S(1)} %get-tuple-element.308), channel_id=1, source_target_pairs={{0,1},{1,2},{2,3},{4,5},{5,6},{6,7},{8,9},{9,10},{10,11},{12,13},{... | collective-permute-start | bytes 393224 | tf_op jit(solution)/shard_map/ppermute | solution.py:23
  66.5 4.4 %collective-permute-start.17 = (f32[2,1,1,128,128]{4,3,2,1,0:T(8,128)S(1)}, f32[2,1,1,128,128]{4,3,2,1,0:T(8,128)S(1)}, u32[]{:S(2)}, u32[]{:S(2)}) collective-permute-start(f32[2,1,1,128,128]{4,3,2,1,0:T(8,128)S(1)} %get-tuple-element.292), channel_id=1, source_target_pairs={{0,1},{1,2},{2,3},{4,5},{5,6},{6,7},{8,9},{9,10},{10,11},{12,13},{... | collective-permute-start | bytes 393224 | tf_op jit(solution)/shard_map/ppermute | solution.py:23
  74.5 4.9 %collective-permute-start.19 = (f32[1,2,128,128]{3,2,1,0:T(8,128)S(1)}, f32[1,2,128,128]{3,2,1,0:T(8,128)S(1)}, u32[]{:S(2)}, u32[]{:S(2)}) collective-permute-start(f32[1,2,128,128]{3,2,1,0:T(8,128)S(1)} %get-tuple-element.282), channel_id=1, source_target_pairs={{0,4},{4,8},{8,12},{12,16},{16,20},{20,24},{24,28},{1,5},{5,9},{9,... | collective-permute-start | bytes 393224 | tf_op jit(solution)/shard_map/ppermute | solution.py:32
  79.6 2.6 %collective-permute-done.19 = f32[1,2,128,128]{3,2,1,0:T(8,128)S(1)} collective-permute-done((f32[1,2,128,128]{3,2,1,0:T(8,128)S(1)}, f32[1,2,128,128]{3,2,1,0:T(8,128)S(1)}, u32[]{:S(2)}, u32[]{:S(2)}) %collective-permute-start.19) | collective-permute-done | bytes 131104 | tf_op jit(solution)/shard_map/ppermute | solution.py:32
  82.3 61.1 %while.10 = (s32[]{:T(128)}, f32[2,1,2,128,128]{4,3,2,1,0:T(8,128)S(1)}, pred[2,1,1,1,1]{0,4,3,2,1:T(4,128)(4,1)S(1)}, f32[2,128,128]{2,1,0:T(8,128)S(1)}, f32[2,1,2,128,128]{4,3,2,1,0:T(8,128)S(1)}, /*index=5*/s32[]{:T(128)}) while((s32[]{:T(128)}, f32[2,1,2,128,128]{4,3,2,1,0:T(8,128)S(1)}, pred[2,1,1,1,1]{0,4,3,2,1:T(4,128)(4,1)S(1)}, ...), condition=%wide.region_1.2_spmd, body=%wide.region_0.1_spmd.sunk | while | flops 2753026 | bytes 12071143 | solution.py:104
  84.3 6.0 %collective-permute-start.1 = (f32[1,2,128,128]{3,2,1,0:T(8,128)}, f32[1,2,128,128]{3,2,1,0:T(8,128)S(1)}, u32[]{:S(2)}, u32[]{:S(2)}) collective-permute-start(f32[1,2,128,128]{3,2,1,0:T(8,128)} %get-tuple-element.398), channel_id=1, source_target_pairs={{0,8},{4,12},{8,16},{12,20},{16,24},{20,28},{1,9},{5,13},{9,17},{1... | collective-permute-start | bytes 393224 | tf_op jit(solution)/shard_map/while/body/eval_jaxpr/ppermute | solution.py:32
  93.4 6.1 %collective-permute-start.2 = (f32[2,1,1,128,128]{4,3,2,1,0:T(8,128)S(1)}, f32[2,1,1,128,128]{4,3,2,1,0:T(8,128)S(1)}, u32[]{:S(2)}, u32[]{:S(2)}) collective-permute-start(f32[2,1,1,128,128]{4,3,2,1,0:T(8,128)S(1)} %get-tuple-element.408), channel_id=1, source_target_pairs={{0,1},{1,2},{2,3},{4,5},{5,6},{6,7},{8,9},{9,10},{10,11},{12,13},{... | collective-permute-start | bytes 393224 | tf_op jit(solution)/shard_map/while/body/eval_jaxpr/ppermute | solution.py:23
  101.7 4.1 %collective-permute-done.3 = f32[2,1,1,128,128]{4,3,2,1,0:T(8,128)S(1)} collective-permute-done((f32[2,1,1,128,128]{4,3,2,1,0:T(8,128)S(1)}, f32[2,1,1,128,128]{4,3,2,1,0:T(8,128)S(1)}, u32[]{:S(2)}, u32[]{:S(2)}) %collective-permute-start.3) | collective-permute-done | bytes 131104 | tf_op jit(solution)/shard_map/while/body/eval_jaxpr/ppermute | solution.py:24
  108.1 4.6 %collective-permute-start.1 = (f32[1,2,128,128]{3,2,1,0:T(8,128)}, f32[1,2,128,128]{3,2,1,0:T(8,128)S(1)}, u32[]{:S(2)}, u32[]{:S(2)}) collective-permute-start(f32[1,2,128,128]{3,2,1,0:T(8,128)} %get-tuple-element.398), channel_id=1, source_target_pairs={{0,8},{4,12},{8,16},{12,20},{16,24},{20,28},{1,9},{5,13},{9,17},{1... | collective-permute-start | bytes 393224 | tf_op jit(solution)/shard_map/while/body/eval_jaxpr/ppermute | solution.py:32
  115.4 2.6 %collective-permute-start.2 = (f32[2,1,1,128,128]{4,3,2,1,0:T(8,128)S(1)}, f32[2,1,1,128,128]{4,3,2,1,0:T(8,128)S(1)}, u32[]{:S(2)}, u32[]{:S(2)}) collective-permute-start(f32[2,1,1,128,128]{4,3,2,1,0:T(8,128)S(1)} %get-tuple-element.408), channel_id=1, source_target_pairs={{0,1},{1,2},{2,3},{4,5},{5,6},{6,7},{8,9},{9,10},{10,11},{12,13},{... | collective-permute-start | bytes 393224 | tf_op jit(solution)/shard_map/while/body/eval_jaxpr/ppermute | solution.py:23
  120.3 4.1 %collective-permute-done.3 = f32[2,1,1,128,128]{4,3,2,1,0:T(8,128)S(1)} collective-permute-done((f32[2,1,1,128,128]{4,3,2,1,0:T(8,128)S(1)}, f32[2,1,1,128,128]{4,3,2,1,0:T(8,128)S(1)}, u32[]{:S(2)}, u32[]{:S(2)}) %collective-permute-start.3) | collective-permute-done | bytes 131104 | tf_op jit(solution)/shard_map/while/body/eval_jaxpr/ppermute | solution.py:24
  126.8 4.6 %collective-permute-start.1 = (f32[1,2,128,128]{3,2,1,0:T(8,128)}, f32[1,2,128,128]{3,2,1,0:T(8,128)S(1)}, u32[]{:S(2)}, u32[]{:S(2)}) collective-permute-start(f32[1,2,128,128]{3,2,1,0:T(8,128)} %get-tuple-element.398), channel_id=1, source_target_pairs={{0,8},{4,12},{8,16},{12,20},{16,24},{20,28},{1,9},{5,13},{9,17},{1... | collective-permute-start | bytes 393224 | tf_op jit(solution)/shard_map/while/body/eval_jaxpr/ppermute | solution.py:32
  134.1 2.6 %collective-permute-start.2 = (f32[2,1,1,128,128]{4,3,2,1,0:T(8,128)S(1)}, f32[2,1,1,128,128]{4,3,2,1,0:T(8,128)S(1)}, u32[]{:S(2)}, u32[]{:S(2)}) collective-permute-start(f32[2,1,1,128,128]{4,3,2,1,0:T(8,128)S(1)} %get-tuple-element.408), channel_id=1, source_target_pairs={{0,1},{1,2},{2,3},{4,5},{5,6},{6,7},{8,9},{9,10},{10,11},{12,13},{... | collective-permute-start | bytes 393224 | tf_op jit(solution)/shard_map/while/body/eval_jaxpr/ppermute | solution.py:23
  139.0 4.1 %collective-permute-done.3 = f32[2,1,1,128,128]{4,3,2,1,0:T(8,128)S(1)} collective-permute-done((f32[2,1,1,128,128]{4,3,2,1,0:T(8,128)S(1)}, f32[2,1,1,128,128]{4,3,2,1,0:T(8,128)S(1)}, u32[]{:S(2)}, u32[]{:S(2)}) %collective-permute-start.3) | collective-permute-done | bytes 131104 | tf_op jit(solution)/shard_map/while/body/eval_jaxpr/ppermute | solution.py:24
  143.4 2.7 %collective-permute-start.20 = (f32[1,2,128,128]{3,2,1,0:T(8,128)S(1)}, f32[1,2,128,128]{3,2,1,0:T(8,128)S(1)}, u32[]{:S(2)}, u32[]{:S(2)}) collective-permute-start(f32[1,2,128,128]{3,2,1,0:T(8,128)S(1)} %get-tuple-element.279), channel_id=1, source_target_pairs={{0,4},{4,8},{8,12},{12,16},{16,20},{20,24},{24,28},{1,5},{5,9},{9,... | collective-permute-start | bytes 393224 | tf_op jit(solution)/shard_map/ppermute | solution.py:32
  147.5 6.1 %collective-permute-start.22 = (f32[1,2,128,128]{3,2,1,0:T(8,128)S(1)}, f32[1,2,128,128]{3,2,1,0:T(8,128)S(1)}, u32[]{:S(2)}, u32[]{:S(2)}) collective-permute-start(f32[1,2,128,128]{3,2,1,0:T(8,128)S(1)} %get-tuple-element.279), channel_id=1, source_target_pairs={{0,8},{4,12},{8,16},{12,20},{16,24},{20,28},{1,9},{5,13},{9,17},{1... | collective-permute-start | bytes 393224 | tf_op jit(solution)/shard_map/ppermute | solution.py:32
  155.5 4.1 %collective-permute-done.23 = f32[1,2,128,128]{3,2,1,0:T(8,128)S(1)} collective-permute-done((f32[1,2,128,128]{3,2,1,0:T(8,128)S(1)}, f32[1,2,128,128]{3,2,1,0:T(8,128)S(1)}, u32[]{:S(2)}, u32[]{:S(2)}) %collective-permute-start.23) | collective-permute-done | bytes 131104 | tf_op jit(solution)/shard_map/ppermute | solution.py:32
  162.3 3.6 %collective-permute-start.25 = (f32[2,1,1,128,128]{4,3,2,1,0:T(8,128)S(1)}, f32[2,1,1,128,128]{4,3,2,1,0:T(8,128)S(1)}, u32[]{:S(2)}, u32[]{:S(2)}) collective-permute-start(f32[2,1,1,128,128]{4,3,2,1,0:T(8,128)S(1)} %get-tuple-element.270), channel_id=1, source_target_pairs={{0,1},{1,2},{2,3},{4,5},{5,6},{6,7},{8,9},{9,10},{10,11},{12,13},{... | collective-permute-start | bytes 393224 | tf_op jit(solution)/shard_map/ppermute | solution.py:23
  170.8 4.4 %collective-permute-start.27 = (f32[2,1,1,128,128]{4,3,2,1,0:T(8,128)S(1)}, f32[2,1,1,128,128]{4,3,2,1,0:T(8,128)S(1)}, u32[]{:S(2)}, u32[]{:S(2)}) collective-permute-start(f32[2,1,1,128,128]{4,3,2,1,0:T(8,128)S(1)} %get-tuple-element.252), channel_id=1, source_target_pairs={{0,1},{1,2},{2,3},{4,5},{5,6},{6,7},{8,9},{9,10},{10,11},{12,13},{... | collective-permute-start | bytes 393224 | tf_op jit(solution)/shard_map/ppermute | solution.py:23
  178.9 4.0 %collective-permute-start.30 = (f32[1,2,128,128]{3,2,1,0:T(8,128)S(1)}, f32[1,2,128,128]{3,2,1,0:T(8,128)S(1)}, u32[]{:S(2)}, u32[]{:S(2)}) collective-permute-start(f32[1,2,128,128]{3,2,1,0:T(8,128)S(1)} %get-tuple-element.241), channel_id=1, source_target_pairs={{0,4},{4,8},{8,12},{12,16},{16,20},{20,24},{24,28},{1,5},{5,9},{9,... | collective-permute-start | bytes 393224 | tf_op jit(solution)/shard_map/ppermute | solution.py:32
  182.9 3.4 %collective-permute-start.28 = (f32[1,2,128,128]{3,2,1,0:T(8,128)S(1)}, f32[1,2,128,128]{3,2,1,0:T(8,128)S(1)}, u32[]{:S(2)}, u32[]{:S(2)}) collective-permute-start(f32[1,2,128,128]{3,2,1,0:T(8,128)S(1)} %get-tuple-element.225), channel_id=1, source_target_pairs={{0,4},{4,8},{8,12},{12,16},{16,20},{20,24},{24,28},{1,5},{5,9},{9,... | collective-permute-start | bytes 393224 | tf_op jit(solution)/shard_map/ppermute | solution.py:32
  190.0 5.2 %collective-permute-start.33 = (f32[2,1,1,128,128]{4,3,2,1,0:T(8,128)S(1)}, f32[2,1,1,128,128]{4,3,2,1,0:T(8,128)S(1)}, u32[]{:S(2)}, u32[]{:S(2)}) collective-permute-start(f32[2,1,1,128,128]{4,3,2,1,0:T(8,128)S(1)} %get-tuple-element.234), channel_id=1, source_target_pairs={{0,1},{1,2},{2,3},{4,5},{5,6},{6,7},{8,9},{9,10},{10,11},{12,13},{... | collective-permute-start | bytes 393224 | tf_op jit(solution)/shard_map/ppermute | solution.py:23
  200.6 4.4 %collective-permute-start.35 = (f32[2,2,1,128,128]{4,3,2,1,0:T(8,128)S(1)}, f32[2,2,1,128,128]{4,3,2,1,0:T(8,128)S(1)}, u32[]{:S(2)}, u32[]{:S(2)}) collective-permute-start(f32[2,2,1,128,128]{4,3,2,1,0:T(8,128)S(1)} %get-tuple-element.144), channel_id=1, source_target_pairs={{0,1},{1,2},{2,3},{4,5},{5,6},{6,7},{8,9},{9,10},{10,11},{12,13},{... | collective-permute-start | bytes 786440 | tf_op jit(solution)/shard_map/ppermute | solution.py:23
  211.8 4.4 %collective-permute-start.37 = (f32[2,2,1,128,128]{4,3,2,1,0:T(8,128)S(1)}, f32[2,2,1,128,128]{4,3,2,1,0:T(8,128)S(1)}, u32[]{:S(2)}, u32[]{:S(2)}) collective-permute-start(f32[2,2,1,128,128]{4,3,2,1,0:T(8,128)S(1)} %get-tuple-element.124), channel_id=1, source_target_pairs={{0,1},{1,2},{2,3},{4,5},{5,6},{6,7},{8,9},{9,10},{10,11},{12,13},{... | collective-permute-start | bytes 786440 | tf_op jit(solution)/shard_map/ppermute | solution.py:23
  223.3 4.4 %collective-permute-start.39 = (f32[2,2,1,128,128]{4,3,2,1,0:T(8,128)S(1)}, f32[2,2,1,128,128]{4,3,2,1,0:T(8,128)S(1)}, u32[]{:S(2)}, u32[]{:S(2)}) collective-permute-start(f32[2,2,1,128,128]{4,3,2,1,0:T(8,128)S(1)} %get-tuple-element.104), channel_id=1, source_target_pairs={{0,1},{1,2},{2,3},{4,5},{5,6},{6,7},{8,9},{9,10},{10,11},{12,13},{... | collective-permute-start | bytes 786440 | tf_op jit(solution)/shard_map/ppermute | solution.py:23
  (297 shorter events, 104.1 us)
Async XLA Ops:
  4.1 8.6 %collective-permute-start.4 = (f32[2,2,1,128,128]{4,3,2,1,0:T(8,128)S(1)}, f32[2,2,1,128,128]{4,3,2,1,0:T(8,128)S(1)}, u32[]{:S(2)}, u32[]{:S(2)}) collective-permute-start(f32[2,2,1,128,128]{4,3,2,1,0:T(8,128)S(1)} %get-tuple-element.213), channel_id=1, source_target_pairs={{1,0},{2,1},{3,2},{5,4},{6,5},{7,6},{9,8},{10,9},{11,10},{13,12},{... | collective-permute-start | bytes 786440 | tf_op jit(solution)/shard_map/ppermute | solution.py:24
  6.1 7.8 %collective-permute-start.5 = (f32[2,2,1,128,128]{4,3,2,1,0:T(8,128)S(1)}, f32[2,2,1,128,128]{4,3,2,1,0:T(8,128)S(1)}, u32[]{:S(2)}, u32[]{:S(2)}) collective-permute-start(f32[2,2,1,128,128]{4,3,2,1,0:T(8,128)S(1)} %get-tuple-element.214), channel_id=1, source_target_pairs={{0,1},{1,2},{2,3},{4,5},{5,6},{6,7},{8,9},{9,10},{10,11},{12,13},{... | collective-permute-start | bytes 786440 | tf_op jit(solution)/shard_map/ppermute | solution.py:23
  15.6 8.4 %collective-permute-start.6 = (f32[2,2,1,128,128]{4,3,2,1,0:T(8,128)S(1)}, f32[2,2,1,128,128]{4,3,2,1,0:T(8,128)S(1)}, u32[]{:S(2)}, u32[]{:S(2)}) collective-permute-start(f32[2,2,1,128,128]{4,3,2,1,0:T(8,128)S(1)} %get-tuple-element.193), channel_id=1, source_target_pairs={{1,0},{2,1},{3,2},{5,4},{6,5},{7,6},{9,8},{10,9},{11,10},{13,12},{... | collective-permute-start | bytes 786440 | tf_op jit(solution)/shard_map/ppermute | solution.py:24
  17.5 7.7 %collective-permute-start.7 = (f32[2,2,1,128,128]{4,3,2,1,0:T(8,128)S(1)}, f32[2,2,1,128,128]{4,3,2,1,0:T(8,128)S(1)}, u32[]{:S(2)}, u32[]{:S(2)}) collective-permute-start(f32[2,2,1,128,128]{4,3,2,1,0:T(8,128)S(1)} %get-tuple-element.194), channel_id=1, source_target_pairs={{0,1},{1,2},{2,3},{4,5},{5,6},{6,7},{8,9},{9,10},{10,11},{12,13},{... | collective-permute-start | bytes 786440 | tf_op jit(solution)/shard_map/ppermute | solution.py:23
  26.9 8.4 %collective-permute-start.8 = (f32[2,2,1,128,128]{4,3,2,1,0:T(8,128)S(1)}, f32[2,2,1,128,128]{4,3,2,1,0:T(8,128)S(1)}, u32[]{:S(2)}, u32[]{:S(2)}) collective-permute-start(f32[2,2,1,128,128]{4,3,2,1,0:T(8,128)S(1)} %get-tuple-element.173), channel_id=1, source_target_pairs={{1,0},{2,1},{3,2},{5,4},{6,5},{7,6},{9,8},{10,9},{11,10},{13,12},{... | collective-permute-start | bytes 786440 | tf_op jit(solution)/shard_map/ppermute | solution.py:24
  28.8 7.7 %collective-permute-start.9 = (f32[2,2,1,128,128]{4,3,2,1,0:T(8,128)S(1)}, f32[2,2,1,128,128]{4,3,2,1,0:T(8,128)S(1)}, u32[]{:S(2)}, u32[]{:S(2)}) collective-permute-start(f32[2,2,1,128,128]{4,3,2,1,0:T(8,128)S(1)} %get-tuple-element.174), channel_id=1, source_target_pairs={{0,1},{1,2},{2,3},{4,5},{5,6},{6,7},{8,9},{9,10},{10,11},{12,13},{... | collective-permute-start | bytes 786440 | tf_op jit(solution)/shard_map/ppermute | solution.py:23
  37.9 7.0 %collective-permute-start.10 = (f32[2,1,1,128,128]{4,3,2,1,0:T(8,128)S(1)}, f32[2,1,1,128,128]{4,3,2,1,0:T(8,128)S(1)}, u32[]{:S(2)}, u32[]{:S(2)}) collective-permute-start(f32[2,1,1,128,128]{4,3,2,1,0:T(8,128)S(1)} %get-tuple-element.325), channel_id=1, source_target_pairs={{1,0},{2,1},{3,2},{5,4},{6,5},{7,6},{9,8},{10,9},{11,10},{13,12},{... | collective-permute-start | bytes 393224 | tf_op jit(solution)/shard_map/ppermute | solution.py:24
  54.8 7.5 %collective-permute-start.14 = (f32[2,1,1,128,128]{4,3,2,1,0:T(8,128)S(1)}, f32[2,1,1,128,128]{4,3,2,1,0:T(8,128)S(1)}, u32[]{:S(2)}, u32[]{:S(2)}) collective-permute-start(f32[2,1,1,128,128]{4,3,2,1,0:T(8,128)S(1)} %get-tuple-element.307), channel_id=1, source_target_pairs={{1,0},{2,1},{3,2},{5,4},{6,5},{7,6},{9,8},{10,9},{11,10},{13,12},{... | collective-permute-start | bytes 393224 | tf_op jit(solution)/shard_map/ppermute | solution.py:24
  56.7 6.8 %collective-permute-start.15 = (f32[2,1,1,128,128]{4,3,2,1,0:T(8,128)S(1)}, f32[2,1,1,128,128]{4,3,2,1,0:T(8,128)S(1)}, u32[]{:S(2)}, u32[]{:S(2)}) collective-permute-start(f32[2,1,1,128,128]{4,3,2,1,0:T(8,128)S(1)} %get-tuple-element.308), channel_id=1, source_target_pairs={{0,1},{1,2},{2,3},{4,5},{5,6},{6,7},{8,9},{9,10},{10,11},{12,13},{... | collective-permute-start | bytes 393224 | tf_op jit(solution)/shard_map/ppermute | solution.py:23
  64.6 7.0 %collective-permute-start.16 = (f32[2,1,1,128,128]{4,3,2,1,0:T(8,128)S(1)}, f32[2,1,1,128,128]{4,3,2,1,0:T(8,128)S(1)}, u32[]{:S(2)}, u32[]{:S(2)}) collective-permute-start(f32[2,1,1,128,128]{4,3,2,1,0:T(8,128)S(1)} %get-tuple-element.291), channel_id=1, source_target_pairs={{1,0},{2,1},{3,2},{5,4},{6,5},{7,6},{9,8},{10,9},{11,10},{13,12},{... | collective-permute-start | bytes 393224 | tf_op jit(solution)/shard_map/ppermute | solution.py:24
  74.5 7.7 %collective-permute-start.19 = (f32[1,2,128,128]{3,2,1,0:T(8,128)S(1)}, f32[1,2,128,128]{3,2,1,0:T(8,128)S(1)}, u32[]{:S(2)}, u32[]{:S(2)}) collective-permute-start(f32[1,2,128,128]{3,2,1,0:T(8,128)S(1)} %get-tuple-element.282), channel_id=1, source_target_pairs={{0,4},{4,8},{8,12},{12,16},{16,20},{20,24},{24,28},{1,5},{5,9},{9,... | collective-permute-start | bytes 393224 | tf_op jit(solution)/shard_map/ppermute | solution.py:32
  83.0 8.0 %collective-permute-start = (f32[1,2,128,128]{3,2,1,0:T(8,128)}, f32[1,2,128,128]{3,2,1,0:T(8,128)S(1)}, u32[]{:S(2)}, u32[]{:S(2)}) collective-permute-start(f32[1,2,128,128]{3,2,1,0:T(8,128)} %get-tuple-element.397), channel_id=1, source_target_pairs={{8,0},{12,4},{16,8},{20,12},{24,16},{28,20},{9,1},{13,5},{17,9},{2... | collective-permute-start | bytes 393224 | tf_op jit(solution)/shard_map/while/body/eval_jaxpr/ppermute | solution.py:32
  84.3 8.6 %collective-permute-start.1 = (f32[1,2,128,128]{3,2,1,0:T(8,128)}, f32[1,2,128,128]{3,2,1,0:T(8,128)S(1)}, u32[]{:S(2)}, u32[]{:S(2)}) collective-permute-start(f32[1,2,128,128]{3,2,1,0:T(8,128)} %get-tuple-element.398), channel_id=1, source_target_pairs={{0,8},{4,12},{8,16},{12,20},{16,24},{20,28},{1,9},{5,13},{9,17},{1... | collective-permute-start | bytes 393224 | tf_op jit(solution)/shard_map/while/body/eval_jaxpr/ppermute | solution.py:32
  93.4 8.3 %collective-permute-start.2 = (f32[2,1,1,128,128]{4,3,2,1,0:T(8,128)S(1)}, f32[2,1,1,128,128]{4,3,2,1,0:T(8,128)S(1)}, u32[]{:S(2)}, u32[]{:S(2)}) collective-permute-start(f32[2,1,1,128,128]{4,3,2,1,0:T(8,128)S(1)} %get-tuple-element.408), channel_id=1, source_target_pairs={{0,1},{1,2},{2,3},{4,5},{5,6},{6,7},{8,9},{9,10},{10,11},{12,13},{... | collective-permute-start | bytes 393224 | tf_op jit(solution)/shard_map/while/body/eval_jaxpr/ppermute | solution.py:23
  108.1 6.8 %collective-permute-start.1 = (f32[1,2,128,128]{3,2,1,0:T(8,128)}, f32[1,2,128,128]{3,2,1,0:T(8,128)S(1)}, u32[]{:S(2)}, u32[]{:S(2)}) collective-permute-start(f32[1,2,128,128]{3,2,1,0:T(8,128)} %get-tuple-element.398), channel_id=1, source_target_pairs={{0,8},{4,12},{8,16},{12,20},{16,24},{20,28},{1,9},{5,13},{9,17},{1... | collective-permute-start | bytes 393224 | tf_op jit(solution)/shard_map/while/body/eval_jaxpr/ppermute | solution.py:32
  126.8 6.8 %collective-permute-start.1 = (f32[1,2,128,128]{3,2,1,0:T(8,128)}, f32[1,2,128,128]{3,2,1,0:T(8,128)S(1)}, u32[]{:S(2)}, u32[]{:S(2)}) collective-permute-start(f32[1,2,128,128]{3,2,1,0:T(8,128)} %get-tuple-element.398), channel_id=1, source_target_pairs={{0,8},{4,12},{8,16},{12,20},{16,24},{20,28},{1,9},{5,13},{9,17},{1... | collective-permute-start | bytes 393224 | tf_op jit(solution)/shard_map/while/body/eval_jaxpr/ppermute | solution.py:32
  143.4 11.5 %collective-permute-start.20 = (f32[1,2,128,128]{3,2,1,0:T(8,128)S(1)}, f32[1,2,128,128]{3,2,1,0:T(8,128)S(1)}, u32[]{:S(2)}, u32[]{:S(2)}) collective-permute-start(f32[1,2,128,128]{3,2,1,0:T(8,128)S(1)} %get-tuple-element.279), channel_id=1, source_target_pairs={{0,4},{4,8},{8,12},{12,16},{16,20},{20,24},{24,28},{1,5},{5,9},{9,... | collective-permute-start | bytes 393224 | tf_op jit(solution)/shard_map/ppermute | solution.py:32
  146.2 8.7 %collective-permute-start.21 = (f32[1,2,128,128]{3,2,1,0:T(8,128)S(1)}, f32[1,2,128,128]{3,2,1,0:T(8,128)S(1)}, u32[]{:S(2)}, u32[]{:S(2)}) collective-permute-start(f32[1,2,128,128]{3,2,1,0:T(8,128)S(1)} %get-tuple-element.280), channel_id=1, source_target_pairs={{4,0},{8,4},{12,8},{16,12},{20,16},{24,20},{28,24},{5,1},{9,5},{13... | collective-permute-start | bytes 393224 | tf_op jit(solution)/shard_map/ppermute | solution.py:32
  147.5 8.0 %collective-permute-start.22 = (f32[1,2,128,128]{3,2,1,0:T(8,128)S(1)}, f32[1,2,128,128]{3,2,1,0:T(8,128)S(1)}, u32[]{:S(2)}, u32[]{:S(2)}) collective-permute-start(f32[1,2,128,128]{3,2,1,0:T(8,128)S(1)} %get-tuple-element.279), channel_id=1, source_target_pairs={{0,8},{4,12},{8,16},{12,20},{16,24},{20,28},{1,9},{5,13},{9,17},{1... | collective-permute-start | bytes 393224 | tf_op jit(solution)/shard_map/ppermute | solution.py:32
  168.9 7.0 %collective-permute-start.26 = (f32[2,1,1,128,128]{4,3,2,1,0:T(8,128)S(1)}, f32[2,1,1,128,128]{4,3,2,1,0:T(8,128)S(1)}, u32[]{:S(2)}, u32[]{:S(2)}) collective-permute-start(f32[2,1,1,128,128]{4,3,2,1,0:T(8,128)S(1)} %get-tuple-element.251), channel_id=1, source_target_pairs={{1,0},{2,1},{3,2},{5,4},{6,5},{7,6},{9,8},{10,9},{11,10},{13,12},{... | collective-permute-start | bytes 393224 | tf_op jit(solution)/shard_map/ppermute | solution.py:24
  177.6 10.0 %collective-permute-start.31 = (f32[1,2,128,128]{3,2,1,0:T(8,128)S(1)}, f32[1,2,128,128]{3,2,1,0:T(8,128)S(1)}, u32[]{:S(2)}, u32[]{:S(2)}) collective-permute-start(f32[1,2,128,128]{3,2,1,0:T(8,128)S(1)} %get-tuple-element.242), channel_id=1, source_target_pairs={{4,0},{8,4},{12,8},{16,12},{20,16},{24,20},{28,24},{5,1},{9,5},{13... | collective-permute-start | bytes 393224 | tf_op jit(solution)/shard_map/ppermute | solution.py:32
  178.9 8.7 %collective-permute-start.30 = (f32[1,2,128,128]{3,2,1,0:T(8,128)S(1)}, f32[1,2,128,128]{3,2,1,0:T(8,128)S(1)}, u32[]{:S(2)}, u32[]{:S(2)}) collective-permute-start(f32[1,2,128,128]{3,2,1,0:T(8,128)S(1)} %get-tuple-element.241), channel_id=1, source_target_pairs={{0,4},{4,8},{8,12},{12,16},{16,20},{20,24},{24,28},{1,5},{5,9},{9,... | collective-permute-start | bytes 393224 | tf_op jit(solution)/shard_map/ppermute | solution.py:32
  182.9 14.6 %collective-permute-start.28 = (f32[1,2,128,128]{3,2,1,0:T(8,128)S(1)}, f32[1,2,128,128]{3,2,1,0:T(8,128)S(1)}, u32[]{:S(2)}, u32[]{:S(2)}) collective-permute-start(f32[1,2,128,128]{3,2,1,0:T(8,128)S(1)} %get-tuple-element.225), channel_id=1, source_target_pairs={{0,4},{4,8},{8,12},{12,16},{16,20},{20,24},{24,28},{1,5},{5,9},{9,... | collective-permute-start | bytes 393224 | tf_op jit(solution)/shard_map/ppermute | solution.py:32
  186.3 11.3 %collective-permute-start.29 = (f32[1,2,128,128]{3,2,1,0:T(8,128)S(1)}, f32[1,2,128,128]{3,2,1,0:T(8,128)S(1)}, u32[]{:S(2)}, u32[]{:S(2)}) collective-permute-start(f32[1,2,128,128]{3,2,1,0:T(8,128)S(1)} %get-tuple-element.226), channel_id=1, source_target_pairs={{4,0},{8,4},{12,8},{16,12},{20,16},{24,20},{28,24},{5,1},{9,5},{13... | collective-permute-start | bytes 393224 | tf_op jit(solution)/shard_map/ppermute | solution.py:32
  188.1 7.8 %collective-permute-start.32 = (f32[2,1,1,128,128]{4,3,2,1,0:T(8,128)S(1)}, f32[2,1,1,128,128]{4,3,2,1,0:T(8,128)S(1)}, u32[]{:S(2)}, u32[]{:S(2)}) collective-permute-start(f32[2,1,1,128,128]{4,3,2,1,0:T(8,128)S(1)} %get-tuple-element.233), channel_id=1, source_target_pairs={{1,0},{2,1},{3,2},{5,4},{6,5},{7,6},{9,8},{10,9},{11,10},{13,12},{... | collective-permute-start | bytes 393224 | tf_op jit(solution)/shard_map/ppermute | solution.py:24
  190.0 7.1 %collective-permute-start.33 = (f32[2,1,1,128,128]{4,3,2,1,0:T(8,128)S(1)}, f32[2,1,1,128,128]{4,3,2,1,0:T(8,128)S(1)}, u32[]{:S(2)}, u32[]{:S(2)}) collective-permute-start(f32[2,1,1,128,128]{4,3,2,1,0:T(8,128)S(1)} %get-tuple-element.234), channel_id=1, source_target_pairs={{0,1},{1,2},{2,3},{4,5},{5,6},{6,7},{8,9},{9,10},{10,11},{12,13},{... | collective-permute-start | bytes 393224 | tf_op jit(solution)/shard_map/ppermute | solution.py:23
  198.6 8.4 %collective-permute-start.34 = (f32[2,2,1,128,128]{4,3,2,1,0:T(8,128)S(1)}, f32[2,2,1,128,128]{4,3,2,1,0:T(8,128)S(1)}, u32[]{:S(2)}, u32[]{:S(2)}) collective-permute-start(f32[2,2,1,128,128]{4,3,2,1,0:T(8,128)S(1)} %get-tuple-element.143), channel_id=1, source_target_pairs={{1,0},{2,1},{3,2},{5,4},{6,5},{7,6},{9,8},{10,9},{11,10},{13,12},{... | collective-permute-start | bytes 786440 | tf_op jit(solution)/shard_map/ppermute | solution.py:24
  200.6 7.7 %collective-permute-start.35 = (f32[2,2,1,128,128]{4,3,2,1,0:T(8,128)S(1)}, f32[2,2,1,128,128]{4,3,2,1,0:T(8,128)S(1)}, u32[]{:S(2)}, u32[]{:S(2)}) collective-permute-start(f32[2,2,1,128,128]{4,3,2,1,0:T(8,128)S(1)} %get-tuple-element.144), channel_id=1, source_target_pairs={{0,1},{1,2},{2,3},{4,5},{5,6},{6,7},{8,9},{9,10},{10,11},{12,13},{... | collective-permute-start | bytes 786440 | tf_op jit(solution)/shard_map/ppermute | solution.py:23
  209.9 8.4 %collective-permute-start.36 = (f32[2,2,1,128,128]{4,3,2,1,0:T(8,128)S(1)}, f32[2,2,1,128,128]{4,3,2,1,0:T(8,128)S(1)}, u32[]{:S(2)}, u32[]{:S(2)}) collective-permute-start(f32[2,2,1,128,128]{4,3,2,1,0:T(8,128)S(1)} %get-tuple-element.123), channel_id=1, source_target_pairs={{1,0},{2,1},{3,2},{5,4},{6,5},{7,6},{9,8},{10,9},{11,10},{13,12},{... | collective-permute-start | bytes 786440 | tf_op jit(solution)/shard_map/ppermute | solution.py:24
  211.8 7.7 %collective-permute-start.37 = (f32[2,2,1,128,128]{4,3,2,1,0:T(8,128)S(1)}, f32[2,2,1,128,128]{4,3,2,1,0:T(8,128)S(1)}, u32[]{:S(2)}, u32[]{:S(2)}) collective-permute-start(f32[2,2,1,128,128]{4,3,2,1,0:T(8,128)S(1)} %get-tuple-element.124), channel_id=1, source_target_pairs={{0,1},{1,2},{2,3},{4,5},{5,6},{6,7},{8,9},{9,10},{10,11},{12,13},{... | collective-permute-start | bytes 786440 | tf_op jit(solution)/shard_map/ppermute | solution.py:23
  221.4 8.4 %collective-permute-start.38 = (f32[2,2,1,128,128]{4,3,2,1,0:T(8,128)S(1)}, f32[2,2,1,128,128]{4,3,2,1,0:T(8,128)S(1)}, u32[]{:S(2)}, u32[]{:S(2)}) collective-permute-start(f32[2,2,1,128,128]{4,3,2,1,0:T(8,128)S(1)} %get-tuple-element.103), channel_id=1, source_target_pairs={{1,0},{2,1},{3,2},{5,4},{6,5},{7,6},{9,8},{10,9},{11,10},{13,12},{... | collective-permute-start | bytes 786440 | tf_op jit(solution)/shard_map/ppermute | solution.py:24
  223.3 7.7 %collective-permute-start.39 = (f32[2,2,1,128,128]{4,3,2,1,0:T(8,128)S(1)}, f32[2,2,1,128,128]{4,3,2,1,0:T(8,128)S(1)}, u32[]{:S(2)}, u32[]{:S(2)}) collective-permute-start(f32[2,2,1,128,128]{4,3,2,1,0:T(8,128)S(1)} %get-tuple-element.104), channel_id=1, source_target_pairs={{0,1},{1,2},{2,3},{4,5},{5,6},{6,7},{8,9},{9,10},{10,11},{12,13},{... | collective-permute-start | bytes 786440 | tf_op jit(solution)/shard_map/ppermute | solution.py:23
  (18 other events, 101.8 us)
where the time goes:
time: 238 us; the launch traced here: 234 us
  starting transfers between devices  145 us (61%)
  waiting for transfers between devices  54.7 us (23%)
  other arithmetic  22.9 us (10%)
  local copies, waits for them, and re-layouts  8.99 us (4%)
    ppermute x15, starting transfers between devices, extended(): before = lax.ppermute(last, axis, up)  64.6 us
    ppermute x18, starting transfers between devices, shifted(): return lax.ppermute(block, axis, route)  52 us
    ppermute x15, starting transfers between devices, extended(): after = lax.ppermute(leading, axis, down)  28.8 us
    ppermute x15, waiting for transfers between devices, extended(): after = lax.ppermute(leading, axis, down)  23.5 us
    ppermute x18, waiting for transfers between devices, shifted(): return lax.ppermute(block, axis, route)  16.8 us
    ppermute x15, waiting for transfers between devices, extended(): before = lax.ppermute(last, axis, up)  14.4 us
    another operation x84, other arithmetic, propagate(): sent = jnp.stack([paired[0], diffusivity * paired[1]])  7.09 us
    sub x15, other arithmetic, second_diff(): return neighbours - 6.0 * centre  5.08 us
  transfers between devices with their start and end apart: 48, of which 39 were waited for; matrix products, arithmetic and copies ran while one was open for 3% of the time, Pallas kernels for 0%

commit v1 on v0

v1 whole, which is shorter than its diff:
```python
import functools
import math

import jax
import jax.numpy as jnp
from jax import lax
from jax.experimental import pallas as pl
from jax.experimental.pallas import tpu as pltpu
from jax.sharding import PartitionSpec as P

YAWS = 24
MESH = pl.DeviceIdType.MESH

tau_levels = (0.03, 0.06, 0.08)
drift_x = 0.3
drift_y = 0.2

HEAD, TAIL = 0, 1
H_R1, T_M1, T_M2 = 12, 13, 14
T_E, T_A1, T_A2, T_A3 = 15, 16, 17, 18
H_E, H_A1 = 19, 20
FINE = 21
EXCHANGES = 29
M1, R1, R2, E_TAIL, E_HEAD = 0, 1, 2, 3, 4


def fine_id(role, block, step):
    return (role * 2 + block) * 3 + step


def late_id(role, block, step):
    return FINE + (role * 2 + block) * 2 + step


def kernel(
    members, slabs,
    yaw, axial, lateral, kappa, source, cotangent,
    forward_out, adjoint_out,
    rhs, points, sent, below, above, own, push, march, resid, stage, passed,
    send_sem, recv_sem, pass_send, pass_recv, in_sem, out_sem,
):
    planes = kappa.shape[0]
    steps = source.shape[0]
    groups = members // 2
    tm, sp = lax.axis_index("tm"), lax.axis_index("space")
    dir_h = lax.rem(tm, 2)
    dir_t = 1 - dir_h
    sign_h = 1 - 2 * dir_h
    sign_t = -sign_h
    pos_h = jnp.where(dir_h == 0, tm, members - 1 - tm)
    g_h = pos_h // 2
    g_t = groups - 1 - g_h
    dirs = (dir_h, dir_t)
    lower, upper = sp > 0, sp < slabs - 1
    first_t, last_t = g_t == 0, g_t == groups - 1
    first_h = g_h == 0

    neighbours = (
        (lower, tm, sp - 1),
        (upper, tm, sp + 1),
        (tm > 0, tm - 1, sp),
        (tm < members - 1, tm + 1, sp),
        (jnp.logical_not(last_t), tm + 2 * sign_t, sp),
        (jnp.logical_not(first_t), tm - 2 * sign_t, sp),
    )
    barrier = pltpu.get_barrier_semaphore()
    count = 0
    for there, t, s in neighbours:
        count = count + there.astype(jnp.int32)

        @pl.when(there)
        def _():
            pl.semaphore_signal(barrier, inc=1, device_id=(t, s), device_id_type=MESH)

    def fetch(direction, j):
        if direction == 0:
            src = source.at[j]
        else:
            src = cotangent.at[steps - 1 - j]
        return pltpu.make_async_copy(src, rhs.at[direction, j], in_sem.at[direction, j])

    for i in range(4):
        for b in range(2):
            fetch(0, 4 * b + i).start()
            fetch(1, 4 * b + i).start()

    ones = jnp.ones(kappa.shape, jnp.float32)
    own[0, 0] = kappa[...]
    own[0, 1] = ones
    own[1, 0] = ones
    own[1, 1] = kappa[...]
    for b in range(2):
        angle = (2.0 * math.pi / YAWS) * jnp.full(kappa.shape[1:], yaw[b], jnp.int32).astype(jnp.float32)
        c, s = jnp.cos(angle[:8]), jnp.sin(angle[:8])
        reps = kappa.shape[1] // 8
        c, s = jnp.concatenate([c] * reps, 0), jnp.concatenate([s] * reps, 0)
        for z in range(planes):
            push[b, z] = c * axial[z] + s * lateral[z]

    nothing = jnp.zeros(below.shape[1:], jnp.float32)

    @pl.when(jnp.logical_not(lower))
    def _():
        def clear(e, carry):
            below[e] = nothing
            return carry
        lax.fori_loop(0, EXCHANGES, clear, 0)

    @pl.when(jnp.logical_not(upper))
    def _():
        def clear(e, carry):
            above[e] = nothing
            return carry
        lax.fori_loop(0, EXCHANGES, clear, 0)

    @pl.when(first_t)
    def _():
        for z in range(planes):
            passed[E_TAIL, z] = nothing

    @pl.when(first_h)
    def _():
        for z in range(planes):
            passed[E_HEAD, z] = nothing

    def rise(e):
        return pltpu.make_async_remote_copy(
            src_ref=sent.at[e, planes - 1], dst_ref=below.at[e],
            send_sem=send_sem.at[e, 0], recv_sem=recv_sem.at[e, 0],
            device_id=(tm, sp + 1), device_id_type=MESH)

    def sink(e):
        return pltpu.make_async_remote_copy(
            src_ref=sent.at[e, 0], dst_ref=above.at[e],
            send_sem=send_sem.at[e, 1], recv_sem=recv_sem.at[e, 1],
            device_id=(tm, sp - 1), device_id_type=MESH)

    def post(e, role, u):
        for z in range(planes):
            sent[e, z] = own[1, dirs[role], z] * u[z]

        @pl.when(upper)
        def _():
            rise(e).start()

        @pl.when(lower)
        def _():
            sink(e).start()

    def arrive(e):
        @pl.when(lower)
        def _():
            rise(e).wait_recv()

        @pl.when(upper)
        def _():
            sink(e).wait_recv()

    at_dest = [1.0 - d.astype(jnp.float32) for d in dirs]
    at_src = [d.astype(jnp.float32) for d in dirs]
    hx, hy = 0.5 * drift_x, 0.5 * drift_y

    def advance(e, role, u, outs):
        d = dirs[role]
        dx, dy = at_dest[role] * hx, at_dest[role] * hy
        sx, sy = at_src[role] * hx, at_src[role] * hy
        rows, cols = u.shape[1:]
        for z in range(planes):
            v, w, a = u[z], sent[e, z], own[0, d, z]
            under = below[e] if z == 0 else sent[e, z - 1]
            over = above[e] if z == planes - 1 else sent[e, z + 1]
            vx, vy = sx * v, sy * v
            total = a * (under + over - 6.0 * w)
            total += (a - dx) * pltpu.roll(w + vx, cols - 1, 1)
            total += (a + dx) * pltpu.roll(w - vx, 1, 1)
            total += (a - dy) * pltpu.roll(w + vy, rows - 1, 0)
            total += (a + dy) * pltpu.roll(w - vy, 1, 0)
            for level, extra, dst in outs:
                dst[z] = v + tau_levels[level] * total + extra[z]

    def emit(direction, j):
        if direction == 0:
            dst = forward_out.at[j]
        else:
            dst = adjoint_out.at[steps - 1 - j]
        return pltpu.make_async_copy(points.at[direction, j], dst, out_sem.at[direction, j])

    def finish(role, j):
        @pl.when(dirs[role] == 0)
        def _():
            emit(0, j).start()

        @pl.when(dirs[role] == 1)
        def _():
            emit(1, j).start()

    def hand(slot, src, distance):
        return pltpu.make_async_remote_copy(
            src_ref=src, dst_ref=passed.at[slot],
            send_sem=pass_send.at[slot], recv_sem=pass_recv.at[slot],
            device_id=(tm + distance, sp), device_id_type=MESH)

    def forcing(role, j):
        return rhs.at[dirs[role], j]

    def point(role, j):
        return points.at[dirs[role], j]

    m1, m2, coarse, t_a1, t_a2 = [stage.at[i] for i in range(5)]

    def load(direction, j):
        fetch(direction, j).wait()
        if direction == 0:
            for z in range(planes):
                rhs[0, j, z] += push[j // 4, z]

    chains = [(HEAD, 0), (HEAD, 1), (TAIL, 0), (TAIL, 1)]
    for b in range(2):
        load(0, 4 * b)
        load(1, 4 * b)
    pl.semaphore_wait(barrier, count)
    for role, b in chains:
        post(fine_id(role, b, 0), role, forcing(role, 4 * b))
    for i in range(1, 4):
        for b in range(2):
            load(0, 4 * b + i)
            load(1, 4 * b + i)
    for i in range(3):
        for role, b in chains:
            e = fine_id(role, b, i)
            u = forcing(role, 4 * b) if i == 0 else march.at[role, b, i - 1]
            dst = resid.at[role, b] if i == 2 else march.at[role, b, i]
            arrive(e)
            advance(e, role, u, [(0, forcing(role, 4 * b + i + 1), dst)])
            if i < 2:
                post(e + 1, role, dst)
            elif (role, b) == (HEAD, 0):
                post(H_R1, HEAD, dst)
    h_r1, h_r2, t_r3, t_r4 = resid.at[HEAD, 0], resid.at[HEAD, 1], resid.at[TAIL, 0], resid.at[TAIL, 1]
    arrive(H_R1)
    advance(H_R1, HEAD, h_r1, [(1, h_r2, m1)])
    partner = sign_h
    hand(M1, m1, partner).start()
    hand(R1, h_r1, partner).start()
    hand(R2, h_r2, partner).start()
    hand(M1, m1, partner).wait_recv()
    post(T_M1, TAIL, passed.at[M1])
    arrive(T_M1)
    advance(T_M1, TAIL, passed.at[M1], [(1, t_r3, m2)])
    post(T_M2, TAIL, m2)
    arrive(T_M2)
    advance(T_M2, TAIL, m2, [(1, t_r4, coarse)])

    e_tail, e_head = passed.at[E_TAIL], passed.at[E_HEAD]
    h_a1, h_a2, t_a3, t_e = point(HEAD, 3), point(HEAD, 7), point(TAIL, 3), point(TAIL, 7)

    def relay():
        @pl.when(jnp.logical_not(last_t))
        def _():
            hand(E_TAIL, t_e, 2 * sign_t).start()
            hand(E_HEAD, t_e, sign_t).start()

    def tail0():
        @pl.when(first_t)
        def _():
            for z in range(planes):
                t_e[z] = coarse[z]
            relay()

        @pl.when(jnp.logical_not(first_t))
        def _():
            hand(E_TAIL, t_e, 2 * sign_t).wait_recv()
        post(T_E, TAIL, e_tail)
        arrive(T_E)

        @pl.when(jnp.logical_not(first_t))
        def _():
            advance(T_E, TAIL, e_tail, [(2, coarse, t_e)])
            relay()
        finish(TAIL, 7)

    def tail1():
        hand(R1, h_r1, partner).wait_recv()
        advance(T_E, TAIL, e_tail, [(1, passed.at[R1], t_a1)])
        post(T_A1, TAIL, t_a1)

    def tail2():
        arrive(T_A1)
        hand(R2, h_r2, partner).wait_recv()
        advance(T_A1, TAIL, t_a1, [(1, passed.at[R2], t_a2)])
        post(T_A2, TAIL, t_a2)

    def tail3():
        arrive(T_A2)
        advance(T_A2, TAIL, t_a2, [(1, t_r3, t_a3), (0, forcing(TAIL, 0), point(TAIL, 0))])
        post(T_A3, TAIL, t_a3)
        post(late_id(TAIL, 0, 0), TAIL, point(TAIL, 0))
        finish(TAIL, 3)
        finish(TAIL, 0)

    def late(role, b, i):
        e = late_id(role, b, i)
        j = 4 * b + i
        arrive(e)
        advance(e, role, point(role, j), [(0, forcing(role, j + 1), point(role, j + 1))])
        if i == 0:
            post(e + 1, role, point(role, j + 1))
        finish(role, j + 1)

    def tail4():
        arrive(T_A3)
        advance(T_A3, TAIL, t_a3, [(0, forcing(TAIL, 4), point(TAIL, 4))])
        post(late_id(TAIL, 1, 0), TAIL, point(TAIL, 4))
        finish(TAIL, 4)
        late(TAIL, 0, 0)

    def tail5():
        late(TAIL, 1, 0)
        late(TAIL, 0, 1)

    def tail6():
        late(TAIL, 1, 1)

    def head0():
        @pl.when(jnp.logical_not(first_h))
        def _():
            hand(E_HEAD, t_e, sign_t).wait_recv()
        post(H_E, HEAD, e_head)
        arrive(H_E)
        advance(H_E, HEAD, e_head, [(1, h_r1, h_a1), (0, forcing(HEAD, 0), point(HEAD, 0))])
        post(H_A1, HEAD, h_a1)
        post(late_id(HEAD, 0, 0), HEAD, point(HEAD, 0))
        finish(HEAD, 3)
        finish(HEAD, 0)

    def head1():
        arrive(H_A1)
        advance(H_A1, HEAD, h_a1, [(0, forcing(HEAD, 4), point(HEAD, 4)), (1, h_r2, h_a2)])
        post(late_id(HEAD, 1, 0), HEAD, point(HEAD, 4))
        finish(HEAD, 4)
        finish(HEAD, 7)
        late(HEAD, 0, 0)

    def head2():
        late(HEAD, 1, 0)
        late(HEAD, 0, 1)

    def head3():
        late(HEAD, 1, 1)

    head_first = g_h < g_t

    @pl.when(head_first)
    def _():
        for part in (head0, head1, tail0, tail1, head2, tail2, head3, tail3, tail4, tail5, tail6):
            part()

    @pl.when(jnp.logical_not(head_first))
    def _():
        for part in (tail0, tail1, tail2, tail3, tail4, head0, tail5, head1, tail6, head2, head3):
            part()

    def settle(e, carry):
        @pl.when(upper)
        def _():
            rise(e).wait_send()

        @pl.when(lower)
        def _():
            sink(e).wait_send()
        return carry

    lax.fori_loop(0, EXCHANGES, settle, 0)
    hand(M1, m1, partner).wait_send()
    hand(R1, h_r1, partner).wait_send()
    hand(R2, h_r2, partner).wait_send()

    @pl.when(jnp.logical_not(last_t))
    def _():
        hand(E_TAIL, t_e, 2 * sign_t).wait_send()
        hand(E_HEAD, t_e, sign_t).wait_send()
    for j in range(steps):
        emit(0, j).wait()
        emit(1, j).wait()


def solution(mesh):
    members, slabs = mesh.shape["tm"], mesh.shape["space"]

    def on_device(source, thrust_axial, thrust_lateral, yaw_index, diffusivity, cotangent):
        steps = source.shape[0]
        slab = diffusivity.shape
        plane = slab[1:]
        vmem = pl.BlockSpec(memory_space=pltpu.VMEM)
        anywhere = pl.BlockSpec(memory_space=pl.ANY)
        f32 = jnp.float32
        return pl.pallas_call(
            functools.partial(kernel, members, slabs),
            out_shape=(jax.ShapeDtypeStruct(source.shape, f32), jax.ShapeDtypeStruct(source.shape, f32)),
            in_specs=[pl.BlockSpec(memory_space=pltpu.SMEM), vmem, vmem, vmem, anywhere, anywhere],
            out_specs=(anywhere, anywhere),
            scratch_shapes=[
                pltpu.VMEM((2, steps) + slab, f32),
                pltpu.VMEM((2, steps) + slab, f32),
                pltpu.VMEM((EXCHANGES,) + slab, f32),
                pltpu.VMEM((EXCHANGES,) + plane, f32),
                pltpu.VMEM((EXCHANGES,) + plane, f32),
                pltpu.VMEM((2, 2) + slab, f32),
                pltpu.VMEM((2,) + slab, f32),
                pltpu.VMEM((2, 2, 2) + slab, f32),
                pltpu.VMEM((2, 2) + slab, f32),
                pltpu.VMEM((5,) + slab, f32),
                pltpu.VMEM((5,) + slab, f32),
                pltpu.SemaphoreType.DMA((EXCHANGES, 2)),
                pltpu.SemaphoreType.DMA((EXCHANGES, 2)),
                pltpu.SemaphoreType.DMA((5,)),
                pltpu.SemaphoreType.DMA((5,)),
                pltpu.SemaphoreType.DMA((2, steps)),
                pltpu.SemaphoreType.DMA((2, steps)),
            ],
            compiler_params=pltpu.CompilerParams(
                collective_id=0, has_side_effects=True, vmem_limit_bytes=40 * 1024 * 1024),
            cost_estimate=pl.CostEstimate(flops=40_000_000, bytes_accessed=4_500_000, transcendentals=0),
        )(yaw_index, thrust_axial, thrust_lateral, diffusivity, source, cotangent)

    return jax.shard_map(
        on_device,
        mesh=mesh,
        in_specs=(
            P("tm", "space", None, None),
            P("space", None, None),
            P("space", None, None),
            P("tm"),
            P("space", None, None),
            P("tm", "space", None, None),
        ),
        out_specs=(P("tm", "space", None, None), P("tm", "space", None, None)),
        check_vma=False,
    )
```

time: 238 us -> 78.2 us (0.33); the launches traced: 234 us -> 77.9 us
  starting transfers between devices: 145 us -> 0 us
  Pallas kernels: 0 us -> 69.5 us
  waiting for transfers between devices: 54.7 us -> 0 us
  other arithmetic: 22.9 us -> 0 us
    ppermute x48 -> x0, starting transfers between devices: 145 us -> none  [the longest x15 64.6 us: extended(): before = lax.ppermute(last, axis, up)]
    pallas_call x0 -> x1, Pallas kernels: none -> 69.5 us  [on_device(): pl.pallas_call(functools.partial(kernel, members, slabs), out_shape=(jax....]
    ppermute x48 -> x0, waiting for transfers between devices: 54.7 us -> none  [the longest x15 23.5 us: extended(): after = lax.ppermute(leading, axis, down)]
    another operation x100 -> x0, other arithmetic: 7.84 us -> none  [the longest x84 7.09 us: propagate(): sent = jnp.stack([paired[0], diffusivity * paired[1]])]
    unnamed x5 -> x14, local copies, waits for them, and re-layouts: 0.03 us -> 7.75 us
    add x32 -> x0, other arithmetic: 7.46 us -> none  [the longest x15 4.24 us: drift(): return 0.5 * drift_x * along_x + 0.5 * drift_y * along_y]
    sub x20 -> x0, other arithmetic: 5.65 us -> none  [the longest x15 5.08 us: second_diff(): return neighbours - 6.0 * centre]
    slice x46 -> x0, local copies, waits for them, and re-layouts: 5.56 us -> none  [the longest x20 3.5 us: drift(): along_x = jnp.roll(field, -1, 4) - jnp.roll(field, 1, 4)]
  transfers between devices with their start and end apart: 48 -> 0, of which waited for: 39 -> 0; matrix products, arithmetic and copies ran while one was open for 3% -> 0% of each run, Pallas kernels for 0% -> 0%
where the time goes in v1:
time: 78.2 us; the launch traced here: 77.9 us
  Pallas kernels  69.5 us (89%)
  local copies, waits for them, and re-layouts  7.75 us (10%)
    pallas_call x1, Pallas kernels, on_device(): pl.pallas_call(functools.partial(kernel, members, slabs), out_shape=(jax....  69.5 us
    unnamed x14, local copies, waits for them, and re-layouts  7.75 us

profile of v1, /device:TPU:1, one launch (start us, length us, event | category | flops | bytes accessed | tf_op | source)
XLA Modules:
  0.0 77.9 jit_solution(8857342111225255562)
XLA Ops:
  0.6 0.0 copy-start
  0.6 1.2 %copy-done = f32[8,2,128,128]{3,2,1,0:T(8,128)S(1)} copy-done((f32[8,2,128,128]{3,2,1,0:T(8,128)S(1)}, f32[8,2,128,128]{3,2,1,0:T(8,128)}, u32[]{:S(2)}) %copy-start) | copy-done | bytes 1048600
  1.9 0.0 copy-start.1
  1.9 1.2 %copy-done.1 = f32[8,2,128,128]{3,2,1,0:T(8,128)S(1)} copy-done((f32[8,2,128,128]{3,2,1,0:T(8,128)S(1)}, f32[8,2,128,128]{3,2,1,0:T(8,128)}, u32[]{:S(2)}) %copy-start.1) | copy-done | bytes 1048600
  3.1 0.0 copy-start.2
  3.1 0.9 %copy-done.2 = f32[2,128,128]{2,1,0:T(8,128)S(1)} copy-done((f32[2,128,128]{2,1,0:T(8,128)S(1)}, f32[2,128,128]{2,1,0:T(8,128)}, u32[]{:S(2)}) %copy-start.2) | copy-done | bytes 131096
  4.0 0.0 copy-start.3
  4.0 0.9 %copy-done.3 = f32[2,128,128]{2,1,0:T(8,128)S(1)} copy-done((f32[2,128,128]{2,1,0:T(8,128)S(1)}, f32[2,128,128]{2,1,0:T(8,128)}, u32[]{:S(2)}) %copy-start.3) | copy-done | bytes 131096
  4.9 0.0 copy-start.4
  4.9 0.9 %copy-done.4 = f32[2,128,128]{2,1,0:T(8,128)S(1)} copy-done((f32[2,128,128]{2,1,0:T(8,128)S(1)}, f32[2,128,128]{2,1,0:T(8,128)}, u32[]{:S(2)}) %copy-start.4) | copy-done | bytes 131096
  5.8 0.0 copy-start.5
  5.8 0.7 copy-done.5
  6.5 69.5 %shard_map.77 = (f32[8,2,128,128]{3,2,1,0:T(8,128)S(1)}, f32[8,2,128,128]{3,2,1,0:T(8,128)S(1)}) custom-call(s32[2]{0:T(128)S(1)} %copy-done.5, f32[2,128,128]{2,1,0:T(8,128)S(1)} %copy-done.2, f32[2,128,128]{2,1,0:T(8,128)S(1)} %copy-done.3, f32[2,128,128]{2,1,0:T(8,128)S(1)} %copy-done.4, f32[8,2,128,128]{3,2,1,0:T(8,128)S(1)} %copy-done, ...), custom_call_target="tpu_custom_call" | custom-call | flops 40000000 | bytes 4500000 | tf_op jit(solution)/shard_map/pallas_call | solution.py:397
  76.0 1.0 %copy.10 = f32[8,2,128,128]{3,2,1,0:T(8,128)} copy(f32[8,2,128,128]{3,2,1,0:T(8,128)S(1)} %get-tuple-element.4) | data formatting | bytes 2097152
  76.9 1.0 %copy.11 = f32[8,2,128,128]{3,2,1,0:T(8,128)} copy(f32[8,2,128,128]{3,2,1,0:T(8,128)S(1)} %get-tuple-element.5) | data formatting | bytes 2097152
Async XLA Ops:
  0.6 1.2 %copy-start = (f32[8,2,128,128]{3,2,1,0:T(8,128)S(1)}, f32[8,2,128,128]{3,2,1,0:T(8,128)}, u32[]{:S(2)}) copy-start(f32[8,2,128,128]{3,2,1,0:T(8,128)} %source.1) | copy-start | bytes 3145732
  1.9 1.2 %copy-start.1 = (f32[8,2,128,128]{3,2,1,0:T(8,128)S(1)}, f32[8,2,128,128]{3,2,1,0:T(8,128)}, u32[]{:S(2)}) copy-start(f32[8,2,128,128]{3,2,1,0:T(8,128)} %cotangent.1) | copy-start | bytes 3145732
  3.1 0.9 %copy-start.2 = (f32[2,128,128]{2,1,0:T(8,128)S(1)}, f32[2,128,128]{2,1,0:T(8,128)}, u32[]{:S(2)}) copy-start(f32[2,128,128]{2,1,0:T(8,128)} %axial.1) | copy-start | bytes 393220
  4.0 0.9 %copy-start.3 = (f32[2,128,128]{2,1,0:T(8,128)S(1)}, f32[2,128,128]{2,1,0:T(8,128)}, u32[]{:S(2)}) copy-start(f32[2,128,128]{2,1,0:T(8,128)} %lateral.1) | copy-start | bytes 393220
  4.9 0.9 %copy-start.4 = (f32[2,128,128]{2,1,0:T(8,128)S(1)}, f32[2,128,128]{2,1,0:T(8,128)}, u32[]{:S(2)}) copy-start(f32[2,128,128]{2,1,0:T(8,128)} %kappa.1) | copy-start | bytes 393220
  5.8 0.7 copy-start.5

commit v2 on v1

--- a/solution.py
+++ b/solution.py
@@ -20,8 +20,8 @@
 T_E, T_A1, T_A2, T_A3 = 15, 16, 17, 18
 H_E, H_A1 = 19, 20
 FINE = 21
-EXCHANGES = 29
-M1, R1, R2, E_TAIL, E_HEAD = 0, 1, 2, 3, 4
+POWERS = 29
+M1, R1, R2 = 0, 1, 2
 
 
 def fine_id(role, block, step):
@@ -34,14 +34,15 @@
 
 def kernel(
     members, slabs,
-    yaw, axial, lateral, kappa, source, cotangent,
+    yaw_hbm, axial_hbm, lateral_hbm, kappa_hbm, source, cotangent,
     forward_out, adjoint_out,
-    rhs, points, sent, below, above, own, push, march, resid, stage, passed,
-    send_sem, recv_sem, pass_send, pass_recv, in_sem, out_sem,
+    yaw, axial, lateral, kappa, rhs, points, sent, below, above, own, push, march, resid, stage, passed, powers, parts,
+    send_sem, recv_sem, pass_send, pass_recv, part_send, part_recv, in_sem, out_sem, small_sem,
 ):
     planes = kappa.shape[0]
     steps = source.shape[0]
     groups = members // 2
+    exchanges = sent.shape[0]
     tm, sp = lax.axis_index("tm"), lax.axis_index("space")
     dir_h = lax.rem(tm, 2)
     dir_t = 1 - dir_h
@@ -52,17 +53,8 @@
     g_t = groups - 1 - g_h
     dirs = (dir_h, dir_t)
     lower, upper = sp > 0, sp < slabs - 1
-    first_t, last_t = g_t == 0, g_t == groups - 1
-    first_h = g_h == 0
-
-    neighbours = (
-        (lower, tm, sp - 1),
-        (upper, tm, sp + 1),
-        (tm > 0, tm - 1, sp),
-        (tm < members - 1, tm + 1, sp),
-        (jnp.logical_not(last_t), tm + 2 * sign_t, sp),
-        (jnp.logical_not(first_t), tm - 2 * sign_t, sp),
-    )
+    neighbours = [(lower, tm, sp - 1), (upper, tm, sp + 1)]
+    neighbours += [(tm != t, t, sp) for t in range(members)]
     barrier = pltpu.get_barrier_semaphore()
     count = 0
     for there, t, s in neighbours:
@@ -79,11 +71,36 @@
             src = cotangent.at[steps - 1 - j]
         return pltpu.make_async_copy(src, rhs.at[direction, j], in_sem.at[direction, j])
 
+    small = [
+        pltpu.make_async_copy(src, dst, small_sem.at[i])
+        for i, (src, dst) in enumerate(
+            ((yaw_hbm, yaw), (kappa_hbm, kappa), (axial_hbm, axial), (lateral_hbm, lateral)))
+    ]
+    for copy in small:
+        copy.start()
     for i in range(4):
         for b in range(2):
             fetch(0, 4 * b + i).start()
             fetch(1, 4 * b + i).start()
 
+    nothing = jnp.zeros(below.shape[1:], jnp.float32)
+
+    @pl.when(jnp.logical_not(lower))
+    def _():
+        def clear(e, carry):
+            below[e] = nothing
+            return carry
+        lax.fori_loop(0, exchanges, clear, 0)
+
+    @pl.when(jnp.logical_not(upper))
+    def _():
+        def clear(e, carry):
+            above[e] = nothing
+            return carry
+        lax.fori_loop(0, exchanges, clear, 0)
+
+    for copy in small:
+        copy.wait()
     ones = jnp.ones(kappa.shape, jnp.float32)
     own[0, 0] = kappa[...]
     own[0, 1] = ones
@@ -96,32 +113,6 @@
         c, s = jnp.concatenate([c] * reps, 0), jnp.concatenate([s] * reps, 0)
         for z in range(planes):
             push[b, z] = c * axial[z] + s * lateral[z]
-
-    nothing = jnp.zeros(below.shape[1:], jnp.float32)
-
-    @pl.when(jnp.logical_not(lower))
-    def _():
-        def clear(e, carry):
-            below[e] = nothing
-            return carry
-        lax.fori_loop(0, EXCHANGES, clear, 0)
-
-    @pl.when(jnp.logical_not(upper))
-    def _():
-        def clear(e, carry):
-            above[e] = nothing
-            return carry
-        lax.fori_loop(0, EXCHANGES, clear, 0)
-
-    @pl.when(first_t)
-    def _():
-        for z in range(planes):
-            passed[E_TAIL, z] = nothing
-
-    @pl.when(first_h)
-    def _():
-        for z in range(planes):
-            passed[E_HEAD, z] = nothing
 
     def rise(e):
         return pltpu.make_async_remote_copy(
@@ -176,7 +167,8 @@
             total += (a - dy) * pltpu.roll(w + vy, rows - 1, 0)
             total += (a + dy) * pltpu.roll(w - vy, 1, 0)
             for level, extra, dst in outs:
-                dst[z] = v + tau_levels[level] * total + extra[z]
+                value = v + tau_levels[level] * total
+                dst[z] = value if extra is None else value + extra[z]
 
     def emit(direction, j):
         if direction == 0:
@@ -206,7 +198,8 @@
     def point(role, j):
         return points.at[dirs[role], j]
 
-    m1, m2, coarse, t_a1, t_a2 = [stage.at[i] for i in range(5)]
+    m1, m2, t_a1, t_a2, e_head, e_tail = [stage.at[i] for i in range(6)]
+    coarse = powers.at[0]
 
     def load(direction, j):
         fetch(direction, j).wait()
@@ -251,38 +244,45 @@
     arrive(T_M2)
     advance(T_M2, TAIL, m2, [(1, t_r4, coarse)])
 
-    e_tail, e_head = passed.at[E_TAIL], passed.at[E_HEAD]
     h_a1, h_a2, t_a3, t_e = point(HEAD, 3), point(HEAD, 7), point(TAIL, 3), point(TAIL, 7)
 
-    def relay():
-        @pl.when(jnp.logical_not(last_t))
-        def _():
-            hand(E_TAIL, t_e, 2 * sign_t).start()
-            hand(E_HEAD, t_e, sign_t).start()
+    def part(role, i):
+        return pltpu.make_async_remote_copy(
+            src_ref=powers.at[i], dst_ref=parts.at[role, i],
+            send_sem=part_send.at[role, i], recv_sem=part_recv.at[role, i],
+            device_id=(tm + sign_t * (2 * i + 1 + role), sp), device_id_type=MESH)
+
+    for i in range(groups - 1):
+        @pl.when(g_t + 1 + i < groups)
+        def _():
+            if i > 0:
+                e = POWERS + i - 1
+                post(e, TAIL, powers.at[i - 1])
+                arrive(e)
+                advance(e, TAIL, powers.at[i - 1], [(2, None, powers.at[i])])
+            part(TAIL, i).start()
+            part(HEAD, i).start()
+
+    def gather(role, group, total):
+        for z in range(planes):
+            total[z] = jnp.zeros(total.shape[1:], jnp.float32)
+        for i in range(groups - 1):
+            @pl.when(i < group)
+            def _():
+                part(role, i).wait_recv()
+                for z in range(planes):
+                    total[z] += parts[role, i, z]
 
     def tail0():
-        @pl.when(first_t)
-        def _():
-            for z in range(planes):
-                t_e[z] = coarse[z]
-            relay()
-
-        @pl.when(jnp.logical_not(first_t))
-        def _():
-            hand(E_TAIL, t_e, 2 * sign_t).wait_recv()
+        gather(TAIL, g_t, e_tail)
         post(T_E, TAIL, e_tail)
+
+    def tail1():
         arrive(T_E)
-
-        @pl.when(jnp.logical_not(first_t))
-        def _():
-            advance(T_E, TAIL, e_tail, [(2, coarse, t_e)])
-            relay()
+        hand(R1, h_r1, partner).wait_recv()
+        advance(T_E, TAIL, e_tail, [(1, passed.at[R1], t_a1), (2, coarse, t_e)])
+        post(T_A1, TAIL, t_a1)
         finish(TAIL, 7)
-
-    def tail1():
-        hand(R1, h_r1, partner).wait_recv()
-        advance(T_E, TAIL, e_tail, [(1, passed.at[R1], t_a1)])
-        post(T_A1, TAIL, t_a1)
 
     def tail2():
         arrive(T_A1)
@@ -322,10 +322,10 @@
         late(TAIL, 1, 1)
 
     def head0():
-        @pl.when(jnp.logical_not(first_h))
-        def _():
-            hand(E_HEAD, t_e, sign_t).wait_recv()
+        gather(HEAD, g_h, e_head)
         post(H_E, HEAD, e_head)
+
+    def head1():
         arrive(H_E)
         advance(H_E, HEAD, e_head, [(1, h_r1, h_a1), (0, forcing(HEAD, 0), point(HEAD, 0))])
         post(H_A1, HEAD, h_a1)
@@ -333,7 +333,7 @@
         finish(HEAD, 3)
         finish(HEAD, 0)
 
-    def head1():
+    def head2():
         arrive(H_A1)
         advance(H_A1, HEAD, h_a1, [(0, forcing(HEAD, 4), point(HEAD, 4)), (1, h_r2, h_a2)])
         post(late_id(HEAD, 1, 0), HEAD, point(HEAD, 4))
@@ -341,23 +341,23 @@
         finish(HEAD, 7)
         late(HEAD, 0, 0)
 
-    def head2():
+    def head3():
         late(HEAD, 1, 0)
         late(HEAD, 0, 1)
 
-    def head3():
+    def head4():
         late(HEAD, 1, 1)
 
     head_first = g_h < g_t
 
     @pl.when(head_first)
     def _():
-        for part in (head0, head1, tail0, tail1, head2, tail2, head3, tail3, tail4, tail5, tail6):
+        for part in (head0, head1, tail0, tail1, head2, tail2, head3, tail3, head4, tail4, tail5, tail6):
             part()
 
     @pl.when(jnp.logical_not(head_first))
     def _():
-        for part in (tail0, tail1, tail2, tail3, tail4, head0, tail5, head1, tail6, head2, head3):
+        for part in (tail0, tail1, tail2, head0, head1, tail3, head2, tail4, head3, tail5, head4, tail6):
             part()
 
     def settle(e, carry):
@@ -370,15 +370,18 @@
             sink(e).wait_send()
         return carry
 
-    lax.fori_loop(0, EXCHANGES, settle, 0)
+    lax.fori_loop(0, POWERS, settle, 0)
     hand(M1, m1, partner).wait_send()
     hand(R1, h_r1, partner).wait_send()
     hand(R2, h_r2, partner).wait_send()
 
-    @pl.when(jnp.logical_not(last_t))
-    def _():
-        hand(E_TAIL, t_e, 2 * sign_t).wait_send()
-        hand(E_HEAD, t_e, sign_t).wait_send()
+    for i in range(groups - 1):
+        @pl.when(g_t + 1 + i < groups)
+        def _():
+            part(TAIL, i).wait_send()
+            part(HEAD, i).wait_send()
+            if i > 0:
+                settle(POWERS + i - 1, 0)
     for j in range(steps):
         emit(0, j).wait()
         emit(1, j).wait()
@@ -389,37 +392,47 @@
 
     def on_device(source, thrust_axial, thrust_lateral, yaw_index, diffusivity, cotangent):
         steps = source.shape[0]
+        links = members // 2 - 1
+        exchanges = POWERS + links - 1
         slab = diffusivity.shape
         plane = slab[1:]
-        vmem = pl.BlockSpec(memory_space=pltpu.VMEM)
         anywhere = pl.BlockSpec(memory_space=pl.ANY)
         f32 = jnp.float32
         return pl.pallas_call(
             functools.partial(kernel, members, slabs),
             out_shape=(jax.ShapeDtypeStruct(source.shape, f32), jax.ShapeDtypeStruct(source.shape, f32)),
-            in_specs=[pl.BlockSpec(memory_space=pltpu.SMEM), vmem, vmem, vmem, anywhere, anywhere],
+            in_specs=[anywhere] * 6,
             out_specs=(anywhere, anywhere),
             scratch_shapes=[
+                pltpu.SMEM(yaw_index.shape, jnp.int32),
+                pltpu.VMEM(slab, f32),
+                pltpu.VMEM(slab, f32),
+                pltpu.VMEM(slab, f32),
                 pltpu.VMEM((2, steps) + slab, f32),
                 pltpu.VMEM((2, steps) + slab, f32),
-                pltpu.VMEM((EXCHANGES,) + slab, f32),
-                pltpu.VMEM((EXCHANGES,) + plane, f32),
-                pltpu.VMEM((EXCHANGES,) + plane, f32),
+                pltpu.VMEM((exchanges,) + slab, f32),
+                pltpu.VMEM((exchanges,) + plane, f32),
+                pltpu.VMEM((exchanges,) + plane, f32),
                 pltpu.VMEM((2, 2) + slab, f32),
                 pltpu.VMEM((2,) + slab, f32),
                 pltpu.VMEM((2, 2, 2) + slab, f32),
                 pltpu.VMEM((2, 2) + slab, f32),
-                pltpu.VMEM((5,) + slab, f32),
-                pltpu.VMEM((5,) + slab, f32),
-                pltpu.SemaphoreType.DMA((EXCHANGES, 2)),
-                pltpu.SemaphoreType.DMA((EXCHANGES, 2)),
-                pltpu.SemaphoreType.DMA((5,)),
-                pltpu.SemaphoreType.DMA((5,)),
+                pltpu.VMEM((6,) + slab, f32),
+                pltpu.VMEM((3,) + slab, f32),
+                pltpu.VMEM((links,) + slab, f32),
+                pltpu.VMEM((2, links) + slab, f32),
+                pltpu.SemaphoreType.DMA((exchanges, 2)),
+                pltpu.SemaphoreType.DMA((exchanges, 2)),
+                pltpu.SemaphoreType.DMA((3,)),
+                pltpu.SemaphoreType.DMA((3,)),
+                pltpu.SemaphoreType.DMA((2, links)),
+                pltpu.SemaphoreType.DMA((2, links)),
                 pltpu.SemaphoreType.DMA((2, steps)),
                 pltpu.SemaphoreType.DMA((2, steps)),
+                pltpu.SemaphoreType.DMA((4,)),
             ],
             compiler_params=pltpu.CompilerParams(
-                collective_id=0, has_side_effects=True, vmem_limit_bytes=40 * 1024 * 1024),
+                collective_id=0, has_side_effects=True, vmem_limit_bytes=60 * 1024 * 1024),
             cost_estimate=pl.CostEstimate(flops=40_000_000, bytes_accessed=4_500_000, transcendentals=0),
         )(yaw_index, thrust_axial, thrust_lateral, diffusivity, source, cotangent)
 

time: 78.2 us -> 73.9 us (0.945)
  local copies, waits for them, and re-layouts: 7.75 us -> 3.36 us
    unnamed x14 -> x4, local copies, waits for them, and re-layouts: 7.75 us -> 3.36 us
where the time goes in v2:
time: 73.9 us; the launch traced here: 73.7 us
  Pallas kernels  69.7 us (94%)
  local copies, waits for them, and re-layouts  3.36 us (5%)
    pallas_call x1, Pallas kernels, on_device(): pl.pallas_call(functools.partial(kernel, members, slabs), out_shape=(jax....  69.7 us
    unnamed x4, local copies, waits for them, and re-layouts  3.36 us

profile of v2, /device:TPU:1, one launch (start us, length us, event | category | flops | bytes accessed | tf_op | source)
XLA Modules:
  0.0 73.7 jit_solution(11133131270945818615)
XLA Ops:
  0.6 69.7 %shard_map.77 = (f32[8,2,128,128]{3,2,1,0:T(8,128)}, f32[8,2,128,128]{3,2,1,0:T(8,128)}) custom-call(s32[2]{0:T(128)} %yaw_hbm.1, f32[2,128,128]{2,1,0:T(8,128)} %axial_hbm.1, f32[2,128,128]{2,1,0:T(8,128)} %lateral_hbm.1, f32[2,128,128]{2,1,0:T(8,128)} %kappa_hbm.1, f32[8,2,128,128]{3,2,1,0:T(8,128)} %source.1, f32[8,2,128,128]{3,2,1,0:T(8,128)} %cotangent.1), custom_call_target="tpu_custom_call" | custom-call | flops 40000000 | bytes 4500000 | tf_op jit(solution)/shard_map/pallas_call | solution.py:401
  70.4 0.0 copy-start
  70.4 2.4 %copy.10 = f32[8,2,128,128]{3,2,1,0:T(8,128)} copy(f32[8,2,128,128]{3,2,1,0:T(8,128)} %get-tuple-element.4) | data formatting | bytes 2097152
  72.8 0.0 copy-done
  72.8 1.0 %copy.11 = f32[8,2,128,128]{3,2,1,0:T(8,128)} copy(f32[8,2,128,128]{3,2,1,0:T(8,128)S(1)} %copy-done) | data formatting | bytes 2097152
Async XLA Ops:
  70.4 2.4 %copy-start = (f32[8,2,128,128]{3,2,1,0:T(8,128)S(1)}, f32[8,2,128,128]{3,2,1,0:T(8,128)}, u32[]{:S(2)}) copy-start(f32[8,2,128,128]{3,2,1,0:T(8,128)} %get-tuple-element.5) | copy-start | bytes 3145732

commit v3 on v2

v3 whole, which is shorter than its diff:
```python
import functools
import math

import jax
import jax.numpy as jnp
from jax import lax
from jax.experimental import pallas as pl
from jax.experimental.pallas import tpu as pltpu
from jax.sharding import PartitionSpec as P

YAWS = 24
MESH = pl.DeviceIdType.MESH

tau_levels = (0.03, 0.06, 0.08)
drift_x = 0.3
drift_y = 0.2

HEAD, TAIL = 0, 1
KAPPA, H_R1, T_R3, T_R1, T_M1, T_E, H_E, T_A2 = range(12, 20)
FIFTH, LATE, POWERS = 20, 22, 26
PAD = 2
M1, R1, R2 = 0, 1, 2


def fine_id(role, block, step):
    return (role * 2 + block) * 3 + step


def kernel(
    members, slabs,
    yaw_hbm, axial_hbm, lateral_hbm, kappa_hbm, source, cotangent,
    forward_out, adjoint_out,
    yaw, axial, lateral, kappa, rhs, points, own, push, march, resid, stage, passed, powers, parts,
    send_sem, recv_sem, pass_send, pass_recv, part_send, part_recv, in_sem, out_sem, small_sem,
):
    planes = kappa.shape[0]
    steps = source.shape[0]
    groups = members // 2
    mid = slice(PAD, PAD + planes)
    mine = pl.ds(PAD, planes)
    tm, sp = lax.axis_index("tm"), lax.axis_index("space")
    dir_h = lax.rem(tm, 2)
    dir_t = 1 - dir_h
    sign_h = 1 - 2 * dir_h
    sign_t = -sign_h
    pos_h = jnp.where(dir_h == 0, tm, members - 1 - tm)
    g_h = pos_h // 2
    g_t = groups - 1 - g_h
    dirs = (dir_h, dir_t)
    lower, upper = sp > 0, sp < slabs - 1
    neighbours = [(lower, tm, sp - 1), (upper, tm, sp + 1)]
    neighbours += [(tm != t, t, sp) for t in range(members)]
    barrier = pltpu.get_barrier_semaphore()
    count = 0
    for there, t, s in neighbours:
        count = count + there.astype(jnp.int32)

        @pl.when(there)
        def _():
            pl.semaphore_signal(barrier, inc=1, device_id=(t, s), device_id_type=MESH)

    def fetch(direction, j):
        if direction == 0:
            src = source.at[j]
        else:
            src = cotangent.at[steps - 1 - j]
        return pltpu.make_async_copy(src, rhs.at[direction, j, mine], in_sem.at[direction, j])

    small = [
        pltpu.make_async_copy(src, dst, small_sem.at[i])
        for i, (src, dst) in enumerate(
            ((yaw_hbm, yaw), (kappa_hbm, kappa), (axial_hbm, axial), (lateral_hbm, lateral)))
    ]
    for copy in small:
        copy.start()
    for i in range(4):
        for b in range(2):
            fetch(0, 4 * b + i).start()
            fetch(1, 4 * b + i).start()

    for copy in small:
        copy.wait()
    wide = own.shape[2:]
    own[0, 1] = jnp.ones(wide, jnp.float32)
    own[1, 0] = jnp.ones(wide, jnp.float32)
    diffuse = own.at[1, 1]
    diffuse[mid] = kappa[...]
    for b in range(2):
        angle = (2.0 * math.pi / YAWS) * jnp.full(kappa.shape[1:], yaw[b], jnp.int32).astype(jnp.float32)
        c, s = jnp.cos(angle[:8]), jnp.sin(angle[:8])
        reps = kappa.shape[1] // 8
        c, s = jnp.concatenate([c] * reps, 0), jnp.concatenate([s] * reps, 0)
        for z in range(planes):
            push[b, z] = c * axial[z] + s * lateral[z]

    def rise(e, ref, depth):
        return pltpu.make_async_remote_copy(
            src_ref=ref.at[pl.ds(PAD + planes - depth, depth)], dst_ref=ref.at[pl.ds(PAD - depth, depth)],
            send_sem=send_sem.at[e, 0], recv_sem=recv_sem.at[e, 0],
            device_id=(tm, sp + 1), device_id_type=MESH)

    def sink(e, ref, depth):
        return pltpu.make_async_remote_copy(
            src_ref=ref.at[pl.ds(PAD, depth)], dst_ref=ref.at[pl.ds(PAD + planes, depth)],
            send_sem=send_sem.at[e, 1], recv_sem=recv_sem.at[e, 1],
            device_id=(tm, sp - 1), device_id_type=MESH)

    posted = {}

    def post(e, ref, depth):
        posted[e] = (ref, depth)
        none = jnp.zeros((depth,) + ref.shape[1:], jnp.float32)

        @pl.when(upper)
        def _():
            rise(e, ref, depth).start()

        @pl.when(jnp.logical_not(upper))
        def _():
            ref[PAD + planes:PAD + planes + depth] = none

        @pl.when(lower)
        def _():
            sink(e, ref, depth).start()

        @pl.when(jnp.logical_not(lower))
        def _():
            ref[PAD - depth:PAD] = none

    def arrive(e):
        ref, depth = posted[e]

        @pl.when(lower)
        def _():
            rise(e, ref, depth).wait_recv()

        @pl.when(upper)
        def _():
            sink(e, ref, depth).wait_recv()

    at_dest = [1.0 - d.astype(jnp.float32) for d in dirs]
    at_src = [d.astype(jnp.float32) for d in dirs]
    hx, hy = 0.5 * drift_x, 0.5 * drift_y

    def advance(role, u, outs, reach=0):
        d = dirs[role]
        dx, dy = at_dest[role] * hx, at_dest[role] * hy
        sx, sy = at_src[role] * hx, at_src[role] * hy
        rows, cols = u.shape[1:]
        for z in range(PAD - reach, PAD + planes + reach):
            v, a = u[z], own[0, d, z]
            w = own[1, d, z] * v
            under = own[1, d, z - 1] * u[z - 1]
            over = own[1, d, z + 1] * u[z + 1]
            vx, vy = sx * v, sy * v
            total = a * (under + over - 6.0 * w)
            total += (a - dx) * pltpu.roll(w + vx, cols - 1, 1)
            total += (a + dx) * pltpu.roll(w - vx, 1, 1)
            total += (a - dy) * pltpu.roll(w + vy, rows - 1, 0)
            total += (a + dy) * pltpu.roll(w - vy, 1, 0)
            for level, extra, dst in outs:
                value = v + tau_levels[level] * total
                dst[z] = value if extra is None else value + extra[z]

    def emit(direction, j):
        if direction == 0:
            dst = forward_out.at[j]
        else:
            dst = adjoint_out.at[steps - 1 - j]
        return pltpu.make_async_copy(points.at[direction, j, mine], dst, out_sem.at[direction, j])

    def finish(role, j):
        @pl.when(dirs[role] == 0)
        def _():
            emit(0, j).start()

        @pl.when(dirs[role] == 1)
        def _():
            emit(1, j).start()

    def hand(slot, src, distance):
        return pltpu.make_async_remote_copy(
            src_ref=src.at[mine], dst_ref=passed.at[slot, mine],
            send_sem=pass_send.at[slot], recv_sem=pass_recv.at[slot],
            device_id=(tm + distance, sp), device_id_type=MESH)

    def forcing(role, j):
        return rhs.at[dirs[role], j]

    def point(role, j):
        return points.at[dirs[role], j]

    m1, m2, t_a1, t_a2, e_head, e_tail = [stage.at[i] for i in range(6)]
    coarse = powers.at[0]

    def load(direction, j):
        fetch(direction, j).wait()
        if direction == 0:
            for z in range(planes):
                rhs[0, j, PAD + z] += push[j // 4, z]

    chains = [(HEAD, 0), (HEAD, 1), (TAIL, 0), (TAIL, 1)]
    for b in range(2):
        load(0, 4 * b)
        load(1, 4 * b)
    pl.semaphore_wait(barrier, count)
    post(KAPPA, diffuse, 2)
    for role, b in chains:
        post(fine_id(role, b, 0), forcing(role, 4 * b), 1)
    for i in range(1, 4):
        for b in range(2):
            load(0, 4 * b + i)
            load(1, 4 * b + i)
    arrive(KAPPA)
    own[0, 0] = diffuse[...]
    for i in range(3):
        for role, b in chains:
            e = fine_id(role, b, i)
            u = forcing(role, 4 * b) if i == 0 else march.at[role, b, i - 1]
            dst = resid.at[role, b] if i == 2 else march.at[role, b, i]
            arrive(e)
            advance(role, u, [(0, forcing(role, 4 * b + i + 1), dst)])
            if i < 2:
                post(e + 1, dst, 1)
            elif b == 0:
                post(H_R1 if role == HEAD else T_R3, dst, 1)
    h_r1, h_r2, t_r3, t_r4 = resid.at[HEAD, 0], resid.at[HEAD, 1], resid.at[TAIL, 0], resid.at[TAIL, 1]
    t_m1, t_r1, t_r2 = passed.at[M1], passed.at[R1], passed.at[R2]
    partner = sign_h
    arrive(H_R1)
    advance(HEAD, h_r1, [(1, h_r2, m1)])
    hand(M1, m1, partner).start()
    hand(R1, h_r1, partner).start()
    hand(R2, h_r2, partner).start()
    for role in (HEAD, TAIL):
        post(FIFTH + role, forcing(role, 5), 1)
    arrive(T_R3)
    hand(M1, m1, partner).wait_recv()
    post(T_M1, t_m1, 2)
    arrive(T_M1)
    advance(TAIL, t_m1, [(1, t_r3, m2)], 1)
    advance(TAIL, m2, [(1, t_r4, coarse)])

    h_a1, h_a2, t_a3, t_e = point(HEAD, 3), point(HEAD, 7), point(TAIL, 3), point(TAIL, 7)

    def part(role, i):
        return pltpu.make_async_remote_copy(
            src_ref=powers.at[i, mine], dst_ref=parts.at[role, i],
            send_sem=part_send.at[role, i], recv_sem=part_recv.at[role, i],
            device_id=(tm + sign_t * (2 * i + 1 + role), sp), device_id_type=MESH)

    for i in range(groups - 1):
        @pl.when(g_t + 1 + i < groups)
        def _():
            if i % 2 == 1:
                e = POWERS + i // 2
                post(e, powers.at[i - 1], 2)
                arrive(e)
                advance(TAIL, powers.at[i - 1], [(2, None, powers.at[i])], 1)
            elif i > 0:
                advance(TAIL, powers.at[i - 1], [(2, None, powers.at[i])])
            part(TAIL, i).start()
            part(HEAD, i).start()

    hand(R1, h_r1, partner).wait_recv()
    post(T_R1, t_r1, 1)

    def gather(role, group, total):
        total[mid] = jnp.zeros((planes,) + total.shape[1:], jnp.float32)
        for i in range(groups - 1):
            @pl.when(i < group)
            def _():
                part(role, i).wait_recv()
                for z in range(planes):
                    total[PAD + z] += parts[role, i, z]

    def tail0():
        gather(TAIL, g_t, e_tail)
        post(T_E, e_tail, 2)

    def tail1():
        arrive(T_R1)
        hand(R2, h_r2, partner).wait_recv()
        arrive(T_E)
        advance(TAIL, e_tail, [(1, t_r1, t_a1)], 1)
        advance(TAIL, t_a1, [(1, t_r2, t_a2)])
        post(T_A2, t_a2, 2)
        advance(TAIL, e_tail, [(2, coarse, t_e)])
        finish(TAIL, 7)

    def tail2():
        arrive(FIFTH + TAIL)
        arrive(T_A2)
        advance(TAIL, t_a2, [(1, t_r3, t_a3), (0, forcing(TAIL, 0), point(TAIL, 0))], 1)
        advance(TAIL, t_a3, [(0, forcing(TAIL, 4), point(TAIL, 4))])
        post(LATE + TAIL * 2, point(TAIL, 4), 2)
        advance(TAIL, point(TAIL, 0), [(0, forcing(TAIL, 1), point(TAIL, 1))])
        post(LATE + TAIL * 2 + 1, point(TAIL, 1), 1)
        for j in (3, 0, 4, 1):
            finish(TAIL, j)

    def last(role):
        arrive(LATE + role * 2)
        advance(role, point(role, 4), [(0, forcing(role, 5), point(role, 5))], 1)
        advance(role, point(role, 5), [(0, forcing(role, 6), point(role, 6))])
        finish(role, 5)
        finish(role, 6)
        arrive(LATE + role * 2 + 1)
        advance(role, point(role, 1), [(0, forcing(role, 2), point(role, 2))])
        finish(role, 2)

    def tail3():
        last(TAIL)

    def head0():
        gather(HEAD, g_h, e_head)
        post(H_E, e_head, 2)

    def head1():
        arrive(FIFTH + HEAD)
        arrive(H_E)
        advance(HEAD, e_head, [(1, h_r1, h_a1), (0, forcing(HEAD, 0), point(HEAD, 0))], 1)
        advance(HEAD, h_a1, [(0, forcing(HEAD, 4), point(HEAD, 4)), (1, h_r2, h_a2)])
        post(LATE + HEAD * 2, point(HEAD, 4), 2)
        advance(HEAD, point(HEAD, 0), [(0, forcing(HEAD, 1), point(HEAD, 1))])
        post(LATE + HEAD * 2 + 1, point(HEAD, 1), 1)
        for j in (3, 0, 4, 7, 1):
            finish(HEAD, j)

    def head2():
        last(HEAD)

    head_first = g_h < g_t

    @pl.when(head_first)
    def _():
        for piece in (head0, head1, tail0, tail1, head2, tail2, tail3):
            piece()

    @pl.when(jnp.logical_not(head_first))
    def _():
        for piece in (tail0, tail1, head0, tail2, head1, tail3, head2):
            piece()

    def settle(e, ref, depth):

        @pl.when(upper)
        def _():
            rise(e, ref, depth).wait_send()

        @pl.when(lower)
        def _():
            sink(e, ref, depth).wait_send()

    for e in range(LATE):
        settle(e, *posted[e])
    for role in (HEAD, TAIL):
        settle(LATE + role * 2, point(role, 4), 2)
        settle(LATE + role * 2 + 1, point(role, 1), 1)
    hand(M1, m1, partner).wait_send()
    hand(R1, h_r1, partner).wait_send()
    hand(R2, h_r2, partner).wait_send()

    for i in range(groups - 1):
        @pl.when(g_t + 1 + i < groups)
        def _():
            part(TAIL, i).wait_send()
            part(HEAD, i).wait_send()
            if i % 2 == 1:
                settle(POWERS + i // 2, powers.at[i - 1], 2)
    for j in range(steps):
        emit(0, j).wait()
        emit(1, j).wait()


def solution(mesh):
    members, slabs = mesh.shape["tm"], mesh.shape["space"]

    def on_device(source, thrust_axial, thrust_lateral, yaw_index, diffusivity, cotangent):
        steps = source.shape[0]
        links = members // 2 - 1
        exchanges = POWERS + max(1, links // 2)
        slab = diffusivity.shape
        wide = (slab[0] + 2 * PAD,) + slab[1:]
        anywhere = pl.BlockSpec(memory_space=pl.ANY)
        f32 = jnp.float32
        return pl.pallas_call(
            functools.partial(kernel, members, slabs),
            out_shape=(jax.ShapeDtypeStruct(source.shape, f32), jax.ShapeDtypeStruct(source.shape, f32)),
            in_specs=[anywhere] * 6,
            out_specs=(anywhere, anywhere),
            scratch_shapes=[
                pltpu.SMEM(yaw_index.shape, jnp.int32),
                pltpu.VMEM(slab, f32),
                pltpu.VMEM(slab, f32),
                pltpu.VMEM(slab, f32),
                pltpu.VMEM((2, steps) + wide, f32),
                pltpu.VMEM((2, steps) + wide, f32),
                pltpu.VMEM((2, 2) + wide, f32),
                pltpu.VMEM((2,) + slab, f32),
                pltpu.VMEM((2, 2, 2) + wide, f32),
                pltpu.VMEM((2, 2) + wide, f32),
                pltpu.VMEM((6,) + wide, f32),
                pltpu.VMEM((3,) + wide, f32),
                pltpu.VMEM((links,) + wide, f32),
                pltpu.VMEM((2, links) + slab, f32),
                pltpu.SemaphoreType.DMA((exchanges, 2)),
                pltpu.SemaphoreType.DMA((exchanges, 2)),
                pltpu.SemaphoreType.DMA((3,)),
                pltpu.SemaphoreType.DMA((3,)),
                pltpu.SemaphoreType.DMA((2, links)),
                pltpu.SemaphoreType.DMA((2, links)),
                pltpu.SemaphoreType.DMA((2, steps)),
                pltpu.SemaphoreType.DMA((2, steps)),
                pltpu.SemaphoreType.DMA((4,)),
            ],
            compiler_params=pltpu.CompilerParams(
                collective_id=0, has_side_effects=True, vmem_limit_bytes=60 * 1024 * 1024),
            cost_estimate=pl.CostEstimate(flops=40_000_000, bytes_accessed=4_500_000, transcendentals=0),
        )(yaw_index, thrust_axial, thrust_lateral, diffusivity, source, cotangent)

    return jax.shard_map(
        on_device,
        mesh=mesh,
        in_specs=(
            P("tm", "space", None, None),
            P("space", None, None),
            P("space", None, None),
            P("tm"),
            P("space", None, None),
            P("tm", "space", None, None),
        ),
        out_specs=(P("tm", "space", None, None), P("tm", "space", None, None)),
        check_vma=False,
    )
```

time: 73.9 us -> 67.9 us (0.919)
  Pallas kernels: 69.7 us -> 63.7 us
    pallas_call x1, Pallas kernels: 69.7 us -> 63.7 us  [on_device(): pl.pallas_call(functools.partial(kernel, members, slabs), out_shape=(jax....]
where the time goes in v3:
time: 67.9 us; the launch traced here: 67.7 us
  Pallas kernels  63.7 us (94%)
  local copies, waits for them, and re-layouts  3.36 us (5%)
    pallas_call x1, Pallas kernels, on_device(): pl.pallas_call(functools.partial(kernel, members, slabs), out_shape=(jax....  63.7 us
    unnamed x4, local copies, waits for them, and re-layouts  3.36 us

profile of v3, /device:TPU:1, one launch (start us, length us, event | category | flops | bytes accessed | tf_op | source)
XLA Modules:
  0.0 67.7 jit_solution(3349204470072752513)
XLA Ops:
  0.6 63.7 %shard_map.77 = (f32[8,2,128,128]{3,2,1,0:T(8,128)}, f32[8,2,128,128]{3,2,1,0:T(8,128)}) custom-call(s32[2]{0:T(128)} %yaw_hbm.1, f32[2,128,128]{2,1,0:T(8,128)} %axial_hbm.1, f32[2,128,128]{2,1,0:T(8,128)} %lateral_hbm.1, f32[2,128,128]{2,1,0:T(8,128)} %kappa_hbm.1, f32[8,2,128,128]{3,2,1,0:T(8,128)} %source.1, f32[8,2,128,128]{3,2,1,0:T(8,128)} %cotangent.1), custom_call_target="tpu_custom_call" | custom-call | flops 40000000 | bytes 4500000 | tf_op jit(solution)/shard_map/pallas_call | solution.py:387
  64.3 0.0 copy-start
  64.3 2.4 %copy.10 = f32[8,2,128,128]{3,2,1,0:T(8,128)} copy(f32[8,2,128,128]{3,2,1,0:T(8,128)} %get-tuple-element.4) | data formatting | bytes 2097152
  66.7 0.0 copy-done
  66.7 1.0 %copy.11 = f32[8,2,128,128]{3,2,1,0:T(8,128)} copy(f32[8,2,128,128]{3,2,1,0:T(8,128)S(1)} %copy-done) | data formatting | bytes 2097152
Async XLA Ops:
  64.3 2.4 %copy-start = (f32[8,2,128,128]{3,2,1,0:T(8,128)S(1)}, f32[8,2,128,128]{3,2,1,0:T(8,128)}, u32[]{:S(2)}) copy-start(f32[8,2,128,128]{3,2,1,0:T(8,128)} %get-tuple-element.5) | copy-start | bytes 3145732

commit v4 on v3

--- a/solution.py
+++ b/solution.py
@@ -19,7 +19,7 @@
 KAPPA, H_R1, T_R3, T_R1, T_M1, T_E, H_E, T_A2 = range(12, 20)
 FIFTH, LATE, POWERS = 20, 22, 26
 PAD = 2
-M1, R1, R2 = 0, 1, 2
+M1, R1, R2, E_HEAD = 0, 1, 2, 3
 
 
 def fine_id(role, block, step):
@@ -49,7 +49,9 @@
     dirs = (dir_h, dir_t)
     lower, upper = sp > 0, sp < slabs - 1
     neighbours = [(lower, tm, sp - 1), (upper, tm, sp + 1)]
-    neighbours += [(tm != t, t, sp) for t in range(members)]
+    for t in range(members):
+        alike = jnp.logical_and(lax.rem(tm + t, 2) == 0, tm != t)
+        neighbours.append((jnp.logical_or(alike, tm + sign_h == t), t, sp))
     barrier = pltpu.get_barrier_semaphore()
     count = 0
     for there, t, s in neighbours:
@@ -190,7 +192,9 @@
     def point(role, j):
         return points.at[dirs[role], j]
 
-    m1, m2, t_a1, t_a2, e_head, e_tail = [stage.at[i] for i in range(6)]
+    m1, m2, t_a1, t_a2, e_tail = [stage.at[i] for i in range(5)]
+    e_head = passed.at[E_HEAD]
+    first_h, first_t = g_h == 0, g_t == 0
     coarse = powers.at[0]
 
     def load(direction, j):
@@ -230,24 +234,24 @@
     arrive(H_R1)
     advance(HEAD, h_r1, [(1, h_r2, m1)])
     hand(M1, m1, partner).start()
-    hand(R1, h_r1, partner).start()
-    hand(R2, h_r2, partner).start()
     for role in (HEAD, TAIL):
         post(FIFTH + role, forcing(role, 5), 1)
     arrive(T_R3)
     hand(M1, m1, partner).wait_recv()
     post(T_M1, t_m1, 2)
+    hand(R1, h_r1, partner).start()
+    hand(R2, h_r2, partner).start()
     arrive(T_M1)
     advance(TAIL, t_m1, [(1, t_r3, m2)], 1)
     advance(TAIL, m2, [(1, t_r4, coarse)])
 
     h_a1, h_a2, t_a3, t_e = point(HEAD, 3), point(HEAD, 7), point(TAIL, 3), point(TAIL, 7)
 
-    def part(role, i):
+    def part(i):
         return pltpu.make_async_remote_copy(
-            src_ref=powers.at[i, mine], dst_ref=parts.at[role, i],
-            send_sem=part_send.at[role, i], recv_sem=part_recv.at[role, i],
-            device_id=(tm + sign_t * (2 * i + 1 + role), sp), device_id_type=MESH)
+            src_ref=powers.at[i, mine], dst_ref=parts.at[i],
+            send_sem=part_send.at[i], recv_sem=part_recv.at[i],
+            device_id=(tm + sign_t * (2 * i + 2), sp), device_id_type=MESH)
 
     for i in range(groups - 1):
         @pl.when(g_t + 1 + i < groups)
@@ -259,24 +263,25 @@
                 advance(TAIL, powers.at[i - 1], [(2, None, powers.at[i])], 1)
             elif i > 0:
                 advance(TAIL, powers.at[i - 1], [(2, None, powers.at[i])])
-            part(TAIL, i).start()
-            part(HEAD, i).start()
+            part(i).start()
 
     hand(R1, h_r1, partner).wait_recv()
     post(T_R1, t_r1, 1)
 
-    def gather(role, group, total):
-        total[mid] = jnp.zeros((planes,) + total.shape[1:], jnp.float32)
+    def tail0():
+        e_tail[mid] = jnp.zeros((planes,) + e_tail.shape[1:], jnp.float32)
         for i in range(groups - 1):
-            @pl.when(i < group)
+            @pl.when(i < g_t)
             def _():
-                part(role, i).wait_recv()
+                part(i).wait_recv()
                 for z in range(planes):
-                    total[PAD + z] += parts[role, i, z]
-
-    def tail0():
-        gather(TAIL, g_t, e_tail)
+                    e_tail[PAD + z] += parts[i, z]
+
         post(T_E, e_tail, 2)
+
+        @pl.when(jnp.logical_not(first_t))
+        def _():
+            hand(E_HEAD, e_tail, partner).start()
 
     def tail1():
         arrive(T_R1)
@@ -313,7 +318,14 @@
         last(TAIL)
 
     def head0():
-        gather(HEAD, g_h, e_head)
+        @pl.when(first_h)
+        def _():
+            e_head[mid] = jnp.zeros((planes,) + e_head.shape[1:], jnp.float32)
+
+        @pl.when(jnp.logical_not(first_h))
+        def _():
+            hand(E_HEAD, e_tail, partner).wait_recv()
+
         post(H_E, e_head, 2)
 
     def head1():
@@ -330,14 +342,12 @@
     def head2():
         last(HEAD)
 
-    head_first = g_h < g_t
-
-    @pl.when(head_first)
+    @pl.when(first_h)
     def _():
         for piece in (head0, head1, tail0, tail1, head2, tail2, tail3):
             piece()
 
-    @pl.when(jnp.logical_not(head_first))
+    @pl.when(jnp.logical_not(first_h))
     def _():
         for piece in (tail0, tail1, head0, tail2, head1, tail3, head2):
             piece()
@@ -361,11 +371,15 @@
     hand(R1, h_r1, partner).wait_send()
     hand(R2, h_r2, partner).wait_send()
 
+    @pl.when(jnp.logical_not(first_t))
+    def _():
+        hand(E_HEAD, e_tail, partner).wait_send()
+
+
     for i in range(groups - 1):
         @pl.when(g_t + 1 + i < groups)
         def _():
-            part(TAIL, i).wait_send()
-            part(HEAD, i).wait_send()
+            part(i).wait_send()
             if i % 2 == 1:
                 settle(POWERS + i // 2, powers.at[i - 1], 2)
     for j in range(steps):
@@ -400,16 +414,16 @@
                 pltpu.VMEM((2,) + slab, f32),
                 pltpu.VMEM((2, 2, 2) + wide, f32),
                 pltpu.VMEM((2, 2) + wide, f32),
-                pltpu.VMEM((6,) + wide, f32),
-                pltpu.VMEM((3,) + wide, f32),
+                pltpu.VMEM((5,) + wide, f32),
+                pltpu.VMEM((4,) + wide, f32),
                 pltpu.VMEM((links,) + wide, f32),
-                pltpu.VMEM((2, links) + slab, f32),
+                pltpu.VMEM((links,) + slab, f32),
                 pltpu.SemaphoreType.DMA((exchanges, 2)),
                 pltpu.SemaphoreType.DMA((exchanges, 2)),
-                pltpu.SemaphoreType.DMA((3,)),
-                pltpu.SemaphoreType.DMA((3,)),
-                pltpu.SemaphoreType.DMA((2, links)),
-                pltpu.SemaphoreType.DMA((2, links)),
+                pltpu.SemaphoreType.DMA((4,)),
+                pltpu.SemaphoreType.DMA((4,)),
+                pltpu.SemaphoreType.DMA((links,)),
+                pltpu.SemaphoreType.DMA((links,)),
                 pltpu.SemaphoreType.DMA((2, steps)),
                 pltpu.SemaphoreType.DMA((2, steps)),
                 pltpu.SemaphoreType.DMA((4,)),

time: 67.9 us -> 57.8 us (0.85)
  Pallas kernels: 63.7 us -> 53.4 us
    pallas_call x1, Pallas kernels: 63.7 us -> 53.4 us  [on_device(): pl.pallas_call(functools.partial(kernel, members, slabs), out_shape=(jax....]
where the time goes in v4:
time: 57.8 us; the launch traced here: 57.4 us
  Pallas kernels  53.4 us (92%)
  local copies, waits for them, and re-layouts  3.36 us (6%)
  between operations  0.65 us (1%)
    pallas_call x1, Pallas kernels, on_device(): pl.pallas_call(functools.partial(kernel, members, slabs), out_shape=(jax....  53.4 us
    unnamed x4, local copies, waits for them, and re-layouts  3.36 us

profile of v4, /device:TPU:1, one launch (start us, length us, event | category | flops | bytes accessed | tf_op | source)
XLA Modules:
  0.0 57.4 jit_solution(3241540898740985880)
XLA Ops:
  0.6 53.4 %shard_map.77 = (f32[8,2,128,128]{3,2,1,0:T(8,128)}, f32[8,2,128,128]{3,2,1,0:T(8,128)}) custom-call(s32[2]{0:T(128)} %yaw_hbm.1, f32[2,128,128]{2,1,0:T(8,128)} %axial_hbm.1, f32[2,128,128]{2,1,0:T(8,128)} %lateral_hbm.1, f32[2,128,128]{2,1,0:T(8,128)} %kappa_hbm.1, f32[8,2,128,128]{3,2,1,0:T(8,128)} %source.1, f32[8,2,128,128]{3,2,1,0:T(8,128)} %cotangent.1), custom_call_target="tpu_custom_call" | custom-call | flops 40000000 | bytes 4500000 | tf_op jit(solution)/shard_map/pallas_call | solution.py:401
  54.1 0.0 copy-start
  54.1 2.4 %copy.10 = f32[8,2,128,128]{3,2,1,0:T(8,128)} copy(f32[8,2,128,128]{3,2,1,0:T(8,128)} %get-tuple-element.4) | data formatting | bytes 2097152
  56.4 0.0 copy-done
  56.5 1.0 %copy.11 = f32[8,2,128,128]{3,2,1,0:T(8,128)} copy(f32[8,2,128,128]{3,2,1,0:T(8,128)S(1)} %copy-done) | data formatting | bytes 2097152
Async XLA Ops:
  54.1 2.4 %copy-start = (f32[8,2,128,128]{3,2,1,0:T(8,128)S(1)}, f32[8,2,128,128]{3,2,1,0:T(8,128)}, u32[]{:S(2)}) copy-start(f32[8,2,128,128]{3,2,1,0:T(8,128)} %get-tuple-element.5) | copy-start | bytes 3145732

commit v5 on v4

--- a/solution.py
+++ b/solution.py
@@ -80,21 +80,6 @@
             fetch(0, 4 * b + i).start()
             fetch(1, 4 * b + i).start()
 
-    for copy in small:
-        copy.wait()
-    wide = own.shape[2:]
-    own[0, 1] = jnp.ones(wide, jnp.float32)
-    own[1, 0] = jnp.ones(wide, jnp.float32)
-    diffuse = own.at[1, 1]
-    diffuse[mid] = kappa[...]
-    for b in range(2):
-        angle = (2.0 * math.pi / YAWS) * jnp.full(kappa.shape[1:], yaw[b], jnp.int32).astype(jnp.float32)
-        c, s = jnp.cos(angle[:8]), jnp.sin(angle[:8])
-        reps = kappa.shape[1] // 8
-        c, s = jnp.concatenate([c] * reps, 0), jnp.concatenate([s] * reps, 0)
-        for z in range(planes):
-            push[b, z] = c * axial[z] + s * lateral[z]
-
     def rise(e, ref, depth):
         return pltpu.make_async_remote_copy(
             src_ref=ref.at[pl.ds(PAD + planes - depth, depth)], dst_ref=ref.at[pl.ds(PAD - depth, depth)],
@@ -204,11 +189,27 @@
                 rhs[0, j, PAD + z] += push[j // 4, z]
 
     chains = [(HEAD, 0), (HEAD, 1), (TAIL, 0), (TAIL, 1)]
+    small[1].wait()
+    wide = own.shape[2:]
+    own[0, 1] = jnp.ones(wide, jnp.float32)
+    own[1, 0] = jnp.ones(wide, jnp.float32)
+    diffuse = own.at[1, 1]
+    diffuse[mid] = kappa[...]
+    pl.semaphore_wait(barrier, count)
+    post(KAPPA, diffuse, 2)
+    for i in (0, 2, 3):
+        small[i].wait()
+    for b in range(2):
+        angle = (2.0 * math.pi / YAWS) * jnp.full(kappa.shape[1:], yaw[b], jnp.int32).astype(jnp.float32)
+        c, s = jnp.cos(angle[:8]), jnp.sin(angle[:8])
+        reps = kappa.shape[1] // 8
+        c, s = jnp.concatenate([c] * reps, 0), jnp.concatenate([s] * reps, 0)
+        for z in range(planes):
+            push[b, z] = c * axial[z] + s * lateral[z]
+
     for b in range(2):
         load(0, 4 * b)
         load(1, 4 * b)
-    pl.semaphore_wait(barrier, count)
-    post(KAPPA, diffuse, 2)
     for role, b in chains:
         post(fine_id(role, b, 0), forcing(role, 4 * b), 1)
     for i in range(1, 4):

time: 57.8 us -> 57.5 us (level)
  no operation moved by 1% of the time
where the time goes in v5:
time: 57.5 us; the launch traced here: 57.1 us
  Pallas kernels  53.1 us (92%)
  local copies, waits for them, and re-layouts  3.36 us (6%)
  between operations  0.65 us (1%)
    pallas_call x1, Pallas kernels, on_device(): pl.pallas_call(functools.partial(kernel, members, slabs), out_shape=(jax....  53.1 us
    unnamed x4, local copies, waits for them, and re-layouts  3.36 us

profile of v5, /device:TPU:1, one launch (start us, length us, event | category | flops | bytes accessed | tf_op | source)
XLA Modules:
  0.0 57.1 jit_solution(3228929739060996142)
XLA Ops:
  0.6 53.1 %shard_map.77 = (f32[8,2,128,128]{3,2,1,0:T(8,128)}, f32[8,2,128,128]{3,2,1,0:T(8,128)}) custom-call(s32[2]{0:T(128)} %yaw_hbm.1, f32[2,128,128]{2,1,0:T(8,128)} %axial_hbm.1, f32[2,128,128]{2,1,0:T(8,128)} %lateral_hbm.1, f32[2,128,128]{2,1,0:T(8,128)} %kappa_hbm.1, f32[8,2,128,128]{3,2,1,0:T(8,128)} %source.1, f32[8,2,128,128]{3,2,1,0:T(8,128)} %cotangent.1), custom_call_target="tpu_custom_call" | custom-call | flops 40000000 | bytes 4500000 | tf_op jit(solution)/shard_map/pallas_call | solution.py:402
  53.8 0.0 copy-start
  53.8 2.4 %copy.10 = f32[8,2,128,128]{3,2,1,0:T(8,128)} copy(f32[8,2,128,128]{3,2,1,0:T(8,128)} %get-tuple-element.4) | data formatting | bytes 2097152
  56.1 0.0 copy-done
  56.2 1.0 %copy.11 = f32[8,2,128,128]{3,2,1,0:T(8,128)} copy(f32[8,2,128,128]{3,2,1,0:T(8,128)S(1)} %copy-done) | data formatting | bytes 2097152
Async XLA Ops:
  53.8 2.4 %copy-start = (f32[8,2,128,128]{3,2,1,0:T(8,128)S(1)}, f32[8,2,128,128]{3,2,1,0:T(8,128)}, u32[]{:S(2)}) copy-start(f32[8,2,128,128]{3,2,1,0:T(8,128)} %get-tuple-element.5) | copy-start | bytes 3145732
